TPU v7x, 256 devices: a whole 4x4x8 slice. The times are simulated.
256 devices in a mesh: dp: 32 (over z, y_lo, core), tensor: 8 (over x, y_hi).
Axes of the slice: x: 4, y: 4 (y_hi: 2, y_lo: 2; y = y_hi * 2 + y_lo), z: 8, core: 2. Of those that a mesh axis runs over, the one named last changes fastest.
Arguments:
- hidden: bfloat16 [32768, 14336], P('dp', 'tensor'), may hold values from -6 to 6
- cotangent: bfloat16 [32768, 4096], P('dp', 'tensor'), may hold values from -0.03125 to 0.03125
- weight_slots: bfloat16 [8, 32, 10, 128, 128], P('tensor', 'dp'), may hold values from -0.0625 to 0.0625
- pattern: int32 [112, 16], P('tensor'), may hold values from 0 to 31, all different within a row
- owners: int32 [112, 16, 1], P('tensor'), may hold values from 0 to 31; in each aligned block of 224 rows (0 to 223, 224 to 447, ..., all dimensions but the last counted through in order) at most 10 rows name the same one
- first_moment: float32 [8, 32, 10, 128, 128], P('tensor', 'dp'), may hold values from -3 to 3
- second_moment: float32 [8, 32, 10, 128, 128], P('tensor', 'dp'), may hold values from 0.05 to 2
- next_hidden: bfloat16 [4096, 14336], P('dp', 'tensor'), may hold values from -6 to 6
Outputs:
- next_out: bfloat16 [4096, 4096], P('dp', 'tensor')
- new_first: float32 [8, 32, 10, 128, 128], P('tensor', 'dp')
- new_second: float32 [8, 32, 10, 128, 128], P('tensor', 'dp')
Inputs may be any that keep to these rules, and one draw needn't show every extreme that they name: `pattern`: each row names 16 different column blocks. `owners`: among the 224 blocks of one tensor index no dp index owns more than 10, and in some tensor index one dp index owns exactly 10.
All inputs are finite; a program needn't handle non-finite values.
Results may differ from a plain program's by a relative error of at most 0.018.
Values may be sent and summed in bfloat16 or wider, within the bound.
A program may use at most 192 MiB of HBM per device.

v0:
```python
import jax
import jax.numpy as jnp
from jax import lax
from jax.sharding import PartitionSpec as P

ADAM_STEP = 20


beta_one = 0.9
beta_two = 0.95
learn_rate = 0.003
epsilon = 1e-08


def slot_tables(owners, dp_devices, slot_limit):
    flat_owner = owners.reshape(-1)
    total_blocks = flat_owner.shape[0]
    member = (flat_owner[:, None] == jnp.arange(dp_devices, dtype=jnp.int32)[None, :]).astype(
        jnp.int32
    )
    before = jnp.cumsum(member, axis=0) - member
    position = jnp.sum(before * member, axis=1)
    target = flat_owner * slot_limit + position
    places = jnp.arange(dp_devices * slot_limit, dtype=jnp.int32)
    matches = (target[None, :] == places[:, None]).astype(jnp.int32)
    source = jnp.sum(matches * jnp.arange(total_blocks, dtype=jnp.int32)[None, :], axis=1)
    filled = jnp.sum(matches, axis=1) > 0
    return (target, source, filled)


def per_device(
    hidden, cotangent, weight_slots, pattern, owners, first_moment, second_moment, next_hidden
):
    tokens_here = hidden.shape[0]
    row_blocks, keep_count = pattern.shape
    block_size = weight_slots.shape[3]
    slot_limit = first_moment.shape[2]
    dp_devices = lax.axis_size("dp")
    my_index = lax.axis_index("dp")
    target, source, filled = slot_tables(owners, dp_devices, slot_limit)
    source_rows = source // keep_count
    source_keeps = source % keep_count
    whole_cot = lax.all_gather(cotangent, "tensor", axis=1, tiled=True)
    column_blocks = whole_cot.shape[1] // block_size
    hidden_blocks = hidden.reshape(tokens_here, row_blocks, block_size)
    cot_blocks = whole_cot.reshape(tokens_here, column_blocks, block_size)

    def keep_term(keep_index):
        selected = cot_blocks[:, pattern[:, keep_index]]
        return jnp.einsum(
            "tfi,tfj->fij", hidden_blocks, selected, preferred_element_type=jnp.float32
        )

    terms = lax.map(keep_term, jnp.arange(keep_count, dtype=jnp.int32))
    outgoing = jnp.where(filled[:, None, None], terms[source_keeps, source_rows], 0.0)
    reduced = lax.psum_scatter(
        outgoing.astype(jnp.bfloat16), "dp", scatter_dimension=0, tiled=True
    ).astype(jnp.float32)
    slot_used = lax.dynamic_slice_in_dim(filled, my_index * slot_limit, slot_limit)[:, None, None]
    old_weights = weight_slots[0, 0].astype(jnp.float32)
    moment_one = first_moment[0, 0]
    moment_two = second_moment[0, 0]
    fresh_one = jnp.where(slot_used, beta_one * moment_one + (1 - beta_one) * reduced, 0.0)
    fresh_two = jnp.where(
        slot_used, beta_two * moment_two + (1 - beta_two) * reduced * reduced, 0.0
    )
    scale_one = 1.0 - beta_one**ADAM_STEP
    scale_two = 1.0 - beta_two**ADAM_STEP
    stepped = old_weights - learn_rate * (fresh_one / scale_one) / (
        jnp.sqrt(fresh_two / scale_two) + epsilon
    )
    new_panels = jnp.where(slot_used, stepped, 0.0).astype(jnp.bfloat16)
    every_panel = lax.all_gather(new_panels, "dp", axis=0, tiled=True)
    packed = every_panel[target].reshape(row_blocks, keep_count, block_size, block_size)
    row_index = jnp.broadcast_to(jnp.arange(row_blocks, dtype=jnp.int32)[:, None], pattern.shape)
    dense = jnp.zeros((row_blocks, column_blocks, block_size, block_size), jnp.bfloat16)
    dense = dense.at[row_index, pattern].set(packed)
    dense = dense.transpose(0, 2, 1, 3).reshape(row_blocks * block_size, column_blocks * block_size)
    flat_out = jnp.dot(next_hidden, dense, preferred_element_type=jnp.float32)
    summed = lax.psum_scatter(
        flat_out.astype(jnp.bfloat16), "tensor", scatter_dimension=1, tiled=True
    )
    return (summed, fresh_one[None, None], fresh_two[None, None])


def solution(mesh):
    in_specs = (
        P("dp", "tensor"),
        P("dp", "tensor"),
        P("tensor", "dp", None, None, None),
        P("tensor", None),
        P("tensor", None, None),
        P("tensor", "dp", None, None, None),
        P("tensor", "dp", None, None, None),
        P("dp", "tensor"),
    )
    out_specs = (
        P("dp", "tensor"),
        P("tensor", "dp", None, None, None),
        P("tensor", "dp", None, None, None),
    )
    return jax.shard_map(
        per_device, mesh=mesh, in_specs=in_specs, out_specs=out_specs, check_vma=False
    )
```

profile of v0, /device:TPU:1, one launch (start us, length us, event | category | flops | bytes accessed | tf_op | source)
XLA Modules:
  0.0 779.9 jit_solution(22290057408831254)
XLA Ops:
  24.3 103.8 %all-gather.3.cloned.1.call-done = bf16[1024,4096]{0,1:T(8,128)(2,1)} async-done(((bf16[1024,512]{0,1:T(8,128)(2,1)}), bf16[1024,4096]{0,1:T(8,128)(2,1)}) %all-gather.3.cloned.1.call-update) | async-done | bytes 8388624 | tf_op jit(solution)/shard_map/all_gather | solution.py:43
  128.1 11.9 %copy.50 = bf16[1024,32,128]{2,0,1:T(8,128)(2,1)} copy(bf16[1024,32,128]{0,2,1:T(8,128)(2,1)} %bitcast.81) | data formatting | bytes 16777216 | tf_op jit(solution)/shard_map/while | solution.py:54
  140.0 229.3 %while.10 = (s32[]{:T(128)}, bf16[16,14,128,128]{3,2,1,0:T(8,128)(2,1)}, s32[16]{0:T(128)S(1)}, s32[14,16]{0,1:T(8,128)S(1)}, bf16[1024,32,128]{2,0,1:T(8,128)(2...) while((s32[]{:T(128)}, bf16[16,14,128,128]{3,2,1,0:T(8,128)(2,1)}, ...), condition=%wide.region_5.6_spmd, body=%wide.region_4.5_spmd.sunk | while | flops 469763104 | bytes 16978300 | solution.py:54
  156.9 6.3 gather_fusion
  185.6 6.3 gather_fusion
  199.9 6.3 gather_fusion
  214.2 6.3 gather_fusion
  228.6 6.3 gather_fusion
  271.6 6.3 gather_fusion
  285.9 6.3 gather_fusion
  300.2 6.3 gather_fusion
  314.5 6.3 gather_fusion
  328.9 6.3 gather_fusion
  343.2 6.3 gather_fusion
  369.3 18.8 %gather_fusion.1 = bf16[320,128,128]{2,1,0:T(8,128)(2,1)} fusion(bf16[16,14,128,128]{3,2,1,0:T(8,128)(2,1)} %get-tuple-element.35, s32[320]{0:T(512)S(1)} %fusion.35), kind=kCustom, calls=%fused_computation.1 | custom fusion | bytes 20974080 | tf_op jit(solution)/shard_map/gather | solution.py:55
  388.1 10.9 %select_convert_fusion = bf16[320,128,128]{2,1,0:T(8,128)(2,1)} fusion(bf16[320,128,128]{2,1,0:T(8,128)(2,1)} %gather_fusion.1, pred[320]{0:T(512)(128)(4,1)S(1)} %broadcast_compare_fusion), kind=kLoop, calls=%fused_computation.11 | loop fusion | flops 5242880 | bytes 20971840 | tf_op jit(solution)/shard_map/convert_element_type | solution.py:57
  399.2 132.9 %reduce-scatter.3.cloned.1.call-done = bf16[10,128,128]{2,1,0:T(8,128)(2,1)} async-done(((bf16[320,128,128]{2,1,0:T(8,128)(2,1)}), bf16[10,128,128]{2,1,0:T(8,128)(2,1)}) %reduce-scatter.3.cloned.1.call-update) | async-done | bytes 327696 | tf_op jit(solution)/shard_map/reduce_scatter | solution.py:56
  535.3 74.7 %all-gather.5.cloned.1.call-done = bf16[320,128,128]{2,1,0:T(8,128)(2,1)} async-done(((bf16[10,128,128]{2,1,0:T(8,128)(2,1)}), bf16[320,128,128]{2,1,0:T(8,128)(2,1)}) %all-gather.5.cloned.1.call-update) | async-done | bytes 10485776 | tf_op jit(solution)/shard_map/all_gather | solution.py:73
  610.0 12.3 %gather_fusion.2 = bf16[224,128,128]{2,1,0:T(8,128)(2,1)} fusion(bf16[320,128,128]{2,1,0:T(8,128)(2,1)} %all-gather.5.cloned.1.call-done, s32[1024]{0:T(1024)S(1)} %pad_clamp_fusion.1), kind=kCustom, calls=%fused_computation.2 | custom fusion | bytes 14680960 | tf_op jit(solution)/shard_map/gather | solution.py:74
  622.4 9.0 %broadcast_in_dim.68 = bf16[14,32,128,128]{3,2,1,0:T(8,128)(2,1)} broadcast(bf16[]{:T(256)} %constant.39.clone.1), dimensions={} | broadcast | bytes 14680066 | tf_op jit(solution)/shard_map/broadcast_in_dim | solution.py:76
  631.3 36.0 %scatter_fusion = bf16[14,32,128,128]{3,2,1,0:T(8,128)(2,1)} fusion(bf16[14,32,128,128]{3,2,1,0:T(8,128)(2,1)} %broadcast_in_dim.68, s32[224]{0:T(256)S(1)} %reshape.212, bf16[224,128,128]{2,1,0:T(8,128)(2,1)} %gather_fusion.2), kind=kCustom, calls=%fused_computation.3 | custom fusion | bytes 22021888 | tf_op jit(solution)/shard_map/scatter | solution.py:77
  667.3 13.3 %copy.53 = bf16[14,128,32,128]{3,2,1,0:T(8,128)(2,1)S(1)} copy(bf16[14,128,32,128]{3,1,2,0:T(8,128)(2,1)} %bitcast.78) | data formatting | bytes 29360128 | tf_op jit(solution)/shard_map/transpose | solution.py:78
  680.6 16.9 %fusion.12 = bf16[128,4096]{0,1:T(8,128)(2,1)} fusion(bf16[128,1792]{1,0:T(8,128)(2,1)S(1)} %copy-done, bf16[224,8,32,128]{3,2,1,0:T(8,128)(2,1)S(1)} %bitcast.79), kind=kOutput, calls=%fused_computation.16 | convolution fusion | flops 1879572480 | bytes 16187392 | tf_op jit(solution)/shard_map/dot_general | solution.py:79
  697.4 74.2 %reduce-scatter.5.cloned.1.call-done = bf16[128,512]{0,1:T(8,128)(2,1)} async-done(((bf16[128,4096]{0,1:T(8,128)(2,1)}), bf16[128,512]{0,1:T(8,128)(2,1)}) %reduce-scatter.5.cloned.1.call-update) | async-done | bytes 131088 | tf_op jit(solution)/shard_map/reduce_scatter | solution.py:80
  (147 shorter events, 150.4 us)
Async XLA Ops:
  7.2 673.4 %copy-start = (bf16[128,1792]{1,0:T(8,128)(2,1)S(1)}, bf16[128,1792]{1,0:T(8,128)(2,1)}, u32[]{:S(2)}) copy-start(bf16[128,1792]{1,0:T(8,128)(2,1)} %param.17) | copy-start | bytes 1376260
  7.2 120.9 %all-gather.3.cloned.1.call-start = ((), (), s32[]{:S(2)}) async-start(), calls=%async_computation.2 | async-start | bytes 9437184 | tf_op jit(solution)/shard_map/all_gather | solution.py:43
  9.6 522.6 %reduce-scatter.3.cloned.1.call-start = ((), (), s32[]{:S(2)}) async-start(), calls=%async_computation.3 | async-start | bytes 10813440 | tf_op jit(solution)/shard_map/reduce_scatter | solution.py:56
  399.1 133.1 %copy-start.1 = (f32[1,1,10,128,128]{4,3,2,1,0:T(8,128)S(1)}, f32[1,1,10,128,128]{4,3,2,1,0:T(8,128)}, u32[]{:S(2)}) copy-start(f32[1,1,10,128,128]{4,3,2,1,0:T(8,128)} %param.16) | copy-start | bytes 1966084
  399.1 133.1 %copy-start.2 = (f32[1,1,10,128,128]{4,3,2,1,0:T(8,128)S(1)}, f32[1,1,10,128,128]{4,3,2,1,0:T(8,128)}, u32[]{:S(2)}) copy-start(f32[1,1,10,128,128]{4,3,2,1,0:T(8,128)} %param.15) | copy-start | bytes 1966084
  399.1 133.1 %copy-start.3 = (bf16[1,1,10,128,128]{4,3,2,1,0:T(8,128)(2,1)S(1)}, bf16[1,1,10,128,128]{4,3,2,1,0:T(8,128)(2,1)}, u32[]{:S(2)}) copy-start(bf16[1,1,10,128,128]{4,3,2,1,0:T(8,128)(2,1)} %param.12) | copy-start | bytes 983044
  399.1 136.1 %copy-start.4 = (s32[14,16]{1,0:T(8,128)S(1)}, s32[14,16]{1,0:T(8,128)}, u32[]{:S(2)}) copy-start(s32[14,16]{1,0:T(8,128)} %param.13) | copy-start | bytes 2692
  399.1 210.9 %all-gather.5.cloned.1.call-start = ((), (), s32[]{:S(2)}) async-start(), calls=%async_computation.4 | async-start | bytes 10813440 | tf_op jit(solution)/shard_map/all_gather | solution.py:73
  534.9 236.8 %reduce-scatter.5.cloned.1.call-start = ((), (), s32[]{:S(2)}) async-start(), calls=%async_computation.5 | async-start | bytes 1179648 | tf_op jit(solution)/shard_map/reduce_scatter | solution.py:80
Sparse Core Ops, SparseCore 0:
  10.6 117.4 all-gather.2
  399.2 132.9 reduce-scatter.2
  535.0 74.9 all-gather.4
  697.6 74.0 reduce-scatter.4
where the time goes:
time: 783 us; the launch traced here: 780 us
  waiting for transfers between devices  386 us (49%)
  local copies, waits for them, and re-layouts  246 us (31%)
  matrix products  86.7 us (11%)
  loops' own time  31.5 us (4%)
  other arithmetic  15.7 us (2%)
  between operations  13.9 us (2%)
    reduce_scatter x1, waiting for transfers between devices, per_device(): lax.psum_scatter(outgoing.astype(jnp.bfloat16), 'dp', scatter_dimension=0...  133 us
    all_gather x1, waiting for transfers between devices, per_device(): whole_cot = lax.all_gather(cotangent, 'tensor', axis=1, tiled=True)  104 us
    gather x16, local copies, waits for them, and re-layouts, keep_term(): selected = cot_blocks[:, pattern[:, keep_index]]  101 us
    all_gather x1, waiting for transfers between devices, per_device(): every_panel = lax.all_gather(new_panels, 'dp', axis=0, tiled=True)  74.7 us
    reduce_scatter x1, waiting for transfers between devices, per_device(): lax.psum_scatter(flat_out.astype(jnp.bfloat16), 'tensor', scatter_dimensi...  74.2 us
    dot_general x16, matrix products, keep_term(): jnp.einsum('tfi,tfj->fij', hidden_blocks, selected, preferred_element_typ...  69.8 us
    scatter x1, local copies, waits for them, and re-layouts, per_device(): dense = dense.at[row_index, pattern].set(packed)  36 us
    another operation x1, loops' own time, per_device(): terms = lax.map(keep_term, jnp.arange(keep_count, dtype=jnp.int32))  31.5 us
  transfers between devices with their start and end apart: 4, of which 4 were waited for; matrix products, arithmetic and copies ran while one was open for 2% of the time, Pallas kernels for 0%

commit v1 on v0

v1 whole, which is shorter than its diff:
```python
import functools

import jax
import jax.numpy as jnp
from jax import lax
from jax.experimental import pallas as pl
from jax.experimental.pallas import tpu as pltpu
from jax.sharding import PartitionSpec as P

ADAM_STEP = 20
BETA_ONE = 0.9
BETA_TWO = 0.95
LEARN_RATE = 0.003
EPSILON = 1e-08

BLK = 128
CHUNKS = 4
MESH = pl.DeviceIdType.MESH
f32 = jnp.float32
bf16 = jnp.bfloat16


def remote(src, dst, send, recv, where):
    return pltpu.make_async_remote_copy(
        src_ref=src, dst_ref=dst, send_sem=send, recv_sem=recv, device_id=where, device_id_type=MESH
    )


def greet(places):
    barrier = pltpu.get_barrier_semaphore()
    for where in places:
        pl.semaphore_signal(barrier, inc=1, device_id=where, device_id_type=MESH)
    pl.semaphore_wait(barrier, len(places))


class Place:
    def __init__(self, nz, nx):
        self.nz, self.nx = nz, nx
        self.d = lax.axis_index("dp")
        self.t = lax.axis_index("tensor")
        self.z = lax.div(self.d, 4)
        self.yl = lax.rem(lax.div(self.d, 2), 2)
        self.core = lax.rem(self.d, 2)
        self.x = lax.div(self.t, 2)
        self.yh = lax.rem(self.t, 2)

    def dp_of(self, z, yl, core):
        return (z * 2 + yl) * 2 + core

    def tensor_of(self, x, yh):
        return x * 2 + yh

    def x_step(self, k):
        return lax.rem(self.x + (k + self.nx), self.nx)

    def z_step(self, k):
        return lax.rem(self.z + (k + self.nz), self.nz)


def grad_kernel(
    nz, nx, slots, row_blocks,
    tab, cnt, hid, cot, wgt, m1, m2,
    new1, new2, panels,
    cotbuf, hid_t, dense, sendb, recvb, ringb, yrecv,
    ys, yr, xs, xr, fs, fr, ds, dr, rs, rr, ls, lr,
):
    me = Place(nz, nx)
    tokens = cot.shape[0]
    rows = tokens // CHUNKS
    half = rows // 2
    n_dense = dense.shape[0] - 1
    hs = slots // 2

    y_far = {"tensor": me.tensor_of(me.x, 1 - me.yh)}
    x_next = [{"tensor": me.tensor_of(me.x_step(1), me.yh)}, {"tensor": me.tensor_of(me.x_step(-1), me.yh)}]
    z_next = [{"dp": me.dp_of(me.z_step(1), me.yl, me.core)}, {"dp": me.dp_of(me.z_step(-1), me.yl, me.core)}]
    y_near = {"dp": me.dp_of(me.z, 1 - me.yl, me.core)}
    twin = {"dp": me.dp_of(me.z, me.yl, 1 - me.core)}
    greet([y_far] + x_next + z_next + [y_near, twin])

    t_item = [me.t, me.tensor_of(me.x, 1 - me.yh)]

    def t_from(item, q):
        yh = me.yh if item == 0 else 1 - me.yh
        return me.tensor_of(me.x_step(-1 if q == 0 else 1), yh)

    def ycopy(c):
        r = pl.ds(c * rows, rows)
        return remote(cot.at[r], cotbuf.at[me.t, r], ys.at[c], yr.at[c], y_far)

    def xcopy(item, q, c):
        r = pl.ds(c * rows, rows)
        src = cot.at[r] if item == 0 else cotbuf.at[t_item[1], r]
        return remote(src, cotbuf.at[t_item[item], r], xs.at[item, q, c], xr.at[item, q, c], x_next[q])

    def fcopy(item, q, c):
        r = pl.ds(c * rows + q * half, half)
        there = cotbuf.at[t_from(item, q), r]
        return remote(there, there, fs.at[item, q, c], fr.at[item, q, c], x_next[q])

    def group(src, tq):
        def body(i, carry):
            out = jnp.dot(hid_t[pl.ds(i * 256, 256), :], src[...], preferred_element_type=f32)
            for b in range(4):
                for a in range(2):
                    dense[(tq * 4 + b) * row_blocks + 2 * i + a] = out[
                        a * BLK : (a + 1) * BLK, b * BLK : (b + 1) * BLK
                    ].astype(bf16)
            return carry

        lax.fori_loop(0, row_blocks // 2, body, 0)

    for c in range(CHUNKS):
        ycopy(c).start()
        for q in range(2):
            xcopy(0, q, c).start()

    for f in range(row_blocks):
        hid_t[f * BLK : (f + 1) * BLK, :] = hid[:, f * BLK : (f + 1) * BLK].T
    dense[n_dense] = jnp.zeros((BLK, BLK), bf16)
    group(cot, me.t)

    for c in range(CHUNKS):
        for q in range(2):
            xcopy(0, q, c).wait_recv()
            fcopy(0, q, c).start()
        ycopy(c).wait_recv()
        for q in range(2):
            xcopy(1, q, c).start()
    group(cotbuf.at[t_from(0, 0)], t_from(0, 0))
    for q in range(2):
        xcopy(1, q, 0).wait_recv()
        fcopy(1, q, 0).start()
    group(cotbuf.at[t_from(0, 1)], t_from(0, 1))
    for q in range(2):
        xcopy(1, q, 1).wait_recv()
        fcopy(1, q, 1).start()
    group(cotbuf.at[t_item[1]], t_item[1])
    for c in range(2, CHUNKS):
        for q in range(2):
            xcopy(1, q, c).wait_recv()
            fcopy(1, q, c).start()
    x_opp = me.x_step(2)
    t_opp = [me.tensor_of(x_opp, me.yh), me.tensor_of(x_opp, 1 - me.yh)]
    for q in range(2):
        for c in range(CHUNKS):
            fcopy(0, q, c).wait_recv()
    group(cotbuf.at[t_opp[0]], t_opp[0])
    for q in range(2):
        group(cotbuf.at[t_from(1, q)], t_from(1, q))
    for q in range(2):
        for c in range(CHUNKS):
            fcopy(1, q, c).wait_recv()
    group(cotbuf.at[t_opp[1]], t_opp[1])

    def dest_z(s, q):
        return lax.rem(me.z + (2 * nz - 1 - s), nz) if q == 0 else lax.rem(me.z + 1 + s, nz)

    def base_of(s, q, u, core):
        yl = 1 - me.yl if u == 0 else me.yl
        return me.dp_of(dest_z(s, q), yl, core) * slots + q * hs

    def dcopy(s, q):
        return remote(sendb.at[s, q], recvb.at[s, q], ds.at[s, q], dr.at[s, q], twin)

    def rcopy(s, q, u):
        return remote(recvb.at[s, q, u], ringb.at[s, q, u], rs.at[s, q, u], rr.at[s, q, u], z_next[q])

    def lcopy(q):
        return remote(recvb.at[nz - 1, q, 0], yrecv.at[q], ls.at[q], lr.at[q], y_near)

    def fill(s, carry):
        for q in range(2):
            for u in range(2):
                base = base_of(s, q, u, 1 - me.core)
                for i in range(hs):
                    sendb[s, q, u, i] = dense[tab[base + i]]
            dcopy(s, q).start()
        return carry

    lax.fori_loop(0, nz, fill, 0)

    def add(s, q, u, first):
        base = base_of(s, q, u, me.core)
        for i in range(hs):
            v = recvb[s, q, u, i].astype(f32) + dense[tab[base + i]].astype(f32)
            if not first:
                v = v + ringb[s - 1, q, u, i].astype(f32)
            recvb[s, q, u, i] = v.astype(bf16)

    for q in range(2):
        dcopy(0, q).wait_recv()
        for u in range(2):
            add(0, q, u, True)
            rcopy(0, q, u).start()

    def ring(s, carry):
        for q in range(2):
            dcopy(s, q).wait_recv()
        for u in range(2):
            for q in range(2):
                rcopy(s - 1, q, u).wait_recv()
                add(s, q, u, False)
                rcopy(s, q, u).start()
        return carry

    lax.fori_loop(1, nz - 1, ring, 0)
    for q in range(2):
        dcopy(nz - 1, q).wait_recv()
    for u in range(2):
        for q in range(2):
            rcopy(nz - 2, q, u).wait_recv()
            add(nz - 1, q, u, False)
            if u == 0:
                lcopy(q).start()

    scale_one = 1.0 - BETA_ONE**ADAM_STEP
    scale_two = 1.0 - BETA_TWO**ADAM_STEP
    mine = cnt[me.d]
    for q in range(2):
        lcopy(q).wait_recv()
        for i in range(hs):
            k = q * hs + i
            grad = recvb[nz - 1, q, 1, i].astype(f32) + yrecv[q, i].astype(f32)
            used = k < mine
            one = jnp.where(used, BETA_ONE * m1[k] + (1 - BETA_ONE) * grad, 0.0)
            two = jnp.where(used, BETA_TWO * m2[k] + (1 - BETA_TWO) * grad * grad, 0.0)
            new1[k] = one
            new2[k] = two
            step = LEARN_RATE * (one / scale_one) / (jnp.sqrt(two / scale_two) + EPSILON)
            panels[k] = (wgt[k].astype(f32) - step).astype(bf16)

    for c in range(CHUNKS):
        ycopy(c).wait_send()
        for q in range(2):
            for item in range(2):
                xcopy(item, q, c).wait_send()
                fcopy(item, q, c).wait_send()
    for q in range(2):
        lcopy(q).wait_send()

    def drain(s, carry):
        for q in range(2):
            dcopy(s, q).wait_send()
        return carry

    def drain_ring(s, carry):
        for q in range(2):
            for u in range(2):
                rcopy(s, q, u).wait_send()
        return carry

    lax.fori_loop(0, nz, drain, 0)
    lax.fori_loop(0, nz - 1, drain_ring, 0)


def next_kernel(
    nz, nx, slots, row_blocks,
    tab, panel, nxt,
    out,
    pan, wide, outb, rcv,
    ys, yr, rs, rr, ds, dr, ts, tr,
):
    me = Place(nz, nx)
    nt = 2 * nx
    hs = slots // 2
    n_pan = nz * 4 * slots

    z_next = [{"dp": me.dp_of(me.z_step(1), me.yl, me.core)}, {"dp": me.dp_of(me.z_step(-1), me.yl, me.core)}]
    y_near = {"dp": me.dp_of(me.z, 1 - me.yl, me.core)}
    twin = {"dp": me.dp_of(me.z, me.yl, 1 - me.core)}
    peers = [{"tensor": lax.rem(me.t + 1 + m, nt)} for m in range(nt - 1)]
    greet(z_next + [y_near, twin] + peers)

    def place(s, q, u):
        z = lax.rem(me.z + (2 * nz - s), nz) if q == 0 else lax.rem(me.z + s, nz)
        yl = me.yl if u == 0 else 1 - me.yl
        return pan.at[pl.ds(me.dp_of(z, yl, me.core) * slots + q * hs, hs)]

    def ycopy(q):
        return remote(panel.at[pl.ds(q * hs, hs)], place(0, q, 0), ys.at[q], yr.at[q], y_near)

    def rcopy(s, q, u):
        here = place(s, q, u)
        src = panel.at[pl.ds(q * hs, hs)] if (isinstance(s, int) and s == 0 and u == 0) else here
        return remote(src, here, rs.at[s, q, u], rr.at[s, q, u], z_next[q])

    def dcopy(s, q, u):
        here = place(s, q, u)
        src = panel.at[pl.ds(q * hs, hs)] if (isinstance(s, int) and s == 0 and u == 0) else here
        return remote(src, here, ds.at[s, q, u], dr.at[s, q, u], twin)

    for q in range(2):
        ycopy(q).start()
        rcopy(0, q, 0).start()
    for q in range(2):
        dcopy(0, q, 0).start()
    for i in range(slots):
        pan[me.d * slots + i] = panel[i]
    pan[n_pan] = jnp.zeros((BLK, BLK), bf16)
    for q in range(2):
        ycopy(q).wait_recv()
        rcopy(0, q, 1).start()
        dcopy(0, q, 1).start()

    def hop(s, carry):
        for u in range(2):
            for q in range(2):
                rcopy(s - 1, q, u).wait_recv()
                rcopy(s, q, u).start()
                dcopy(s, q, u).start()
        return carry

    lax.fori_loop(1, nz - 1, hop, 0)
    for u in range(2):
        for q in range(2):
            rcopy(nz - 2, q, u).wait_recv()
            dcopy(nz - 1, q, u).start()

    def landed(s, carry):
        for u in range(2):
            for q in range(2):
                dcopy(s, q, u).wait_recv()
        return carry

    lax.fori_loop(0, nz, landed, 0)

    def tcopy(m):
        return remote(outb.at[m], rcv.at[m], ts.at[m], tr.at[m], peers[m])

    total = None
    for m in range(nt):
        tq = lax.rem(me.t + 1 + m, nt)
        buf = m % 2

        def build(f, carry):
            for b in range(4):
                wide[buf, pl.ds(f * BLK, BLK), b * BLK : (b + 1) * BLK] = pan[tab[(tq * 4 + b) * row_blocks + f]]
            return carry

        lax.fori_loop(0, row_blocks, build, 0)
        part = jnp.dot(nxt[...], wide[buf], preferred_element_type=f32)
        if m < nt - 1:
            outb[m] = part.astype(bf16)
            tcopy(m).start()
        else:
            total = part
    for m in range(nt - 1):
        tcopy(m).wait_recv()
        total = total + rcv[m].astype(f32)
    out[...] = total.astype(bf16)

    for m in range(nt - 1):
        tcopy(m).wait_send()
    for q in range(2):
        ycopy(q).wait_send()

    def drain(s, carry):
        for u in range(2):
            for q in range(2):
                dcopy(s, q, u).wait_send()
        return carry

    def drain_ring(s, carry):
        for u in range(2):
            for q in range(2):
                rcopy(s, q, u).wait_send()
        return carry

    lax.fori_loop(0, nz, drain, 0)
    lax.fori_loop(0, nz - 1, drain_ring, 0)


def tables(pattern, owners, dp_devices, slots, row_blocks, col_blocks):
    keep = pattern.shape[1]
    total = row_blocks * keep
    owner = owners.reshape(total)
    number = jnp.arange(total, dtype=jnp.int32)
    same = owner[:, None] == owner[None, :]
    earlier = number[None, :] < number[:, None]
    position = jnp.sum((same & earlier).astype(jnp.int32), axis=1)
    target = owner * slots + position
    where = pattern.reshape(total) * row_blocks + number // keep
    places = jnp.arange(dp_devices * slots, dtype=jnp.int32)
    hit = target[None, :] == places[:, None]
    n_dense = row_blocks * col_blocks
    grad_tab = n_dense + jnp.sum(jnp.where(hit, where[None, :] - n_dense, 0), axis=1)
    spots = jnp.arange(n_dense, dtype=jnp.int32)
    found = where[None, :] == spots[:, None]
    n_pan = dp_devices * slots
    next_tab = n_pan + jnp.sum(jnp.where(found, target[None, :] - n_pan, 0), axis=1)
    people = jnp.arange(dp_devices, dtype=jnp.int32)
    count = jnp.sum((owner[None, :] == people[:, None]).astype(jnp.int32), axis=1)
    return grad_tab, next_tab, count


def per_device(hidden, cotangent, weight_slots, pattern, owners, first_moment, second_moment, next_hidden):
    tokens, width = hidden.shape
    cols = cotangent.shape[1]
    row_blocks = pattern.shape[0]
    slots = first_moment.shape[2]
    n_dp, n_t = lax.axis_size("dp"), lax.axis_size("tensor")
    nz, nx = n_dp // 4, n_t // 2
    col_blocks = cols * n_t // BLK
    hs = slots // 2
    grad_tab, next_tab, count = tables(pattern, owners, n_dp, slots, row_blocks, col_blocks)

    vmem = pl.BlockSpec(memory_space=pltpu.VMEM)
    smem = pl.BlockSpec(memory_space=pltpu.SMEM)
    dma = pltpu.SemaphoreType.DMA
    block = (slots, BLK, BLK)
    new1, new2, panels = pl.pallas_call(
        functools.partial(grad_kernel, nz, nx, slots, row_blocks),
        out_shape=(
            jax.ShapeDtypeStruct(block, f32),
            jax.ShapeDtypeStruct(block, f32),
            jax.ShapeDtypeStruct(block, bf16),
        ),
        in_specs=[smem, smem] + [vmem] * 5,
        out_specs=(vmem, vmem, vmem),
        scratch_shapes=[
            pltpu.VMEM((n_t, tokens, cols), bf16),
            pltpu.VMEM((width, tokens), bf16),
            pltpu.VMEM((row_blocks * col_blocks + 1, BLK, BLK), bf16),
            pltpu.VMEM((nz, 2, 2, hs, BLK, BLK), bf16),
            pltpu.VMEM((nz, 2, 2, hs, BLK, BLK), bf16),
            pltpu.VMEM((nz - 1, 2, 2, hs, BLK, BLK), bf16),
            pltpu.VMEM((2, hs, BLK, BLK), bf16),
            dma((CHUNKS,)),
            dma((CHUNKS,)),
            dma((2, 2, CHUNKS)),
            dma((2, 2, CHUNKS)),
            dma((2, 2, CHUNKS)),
            dma((2, 2, CHUNKS)),
            dma((nz, 2)),
            dma((nz, 2)),
            dma((nz - 1, 2, 2)),
            dma((nz - 1, 2, 2)),
            dma((2,)),
            dma((2,)),
        ],
        compiler_params=pltpu.CompilerParams(
            collective_id=0, has_side_effects=True, vmem_limit_bytes=60 * 1024 * 1024
        ),
        name="grad_adam",
    )(grad_tab, count, hidden, cotangent, weight_slots[0, 0], first_moment[0, 0], second_moment[0, 0])

    next_out = pl.pallas_call(
        functools.partial(next_kernel, nz, nx, slots, row_blocks),
        out_shape=jax.ShapeDtypeStruct((next_hidden.shape[0], cols), bf16),
        in_specs=[smem, vmem, vmem],
        out_specs=vmem,
        scratch_shapes=[
            pltpu.VMEM((n_dp * slots + 1, BLK, BLK), bf16),
            pltpu.VMEM((2, width, cols), bf16),
            pltpu.VMEM((n_t - 1, next_hidden.shape[0], cols), bf16),
            pltpu.VMEM((n_t - 1, next_hidden.shape[0], cols), bf16),
            dma((2,)),
            dma((2,)),
            dma((nz - 1, 2, 2)),
            dma((nz - 1, 2, 2)),
            dma((nz, 2, 2)),
            dma((nz, 2, 2)),
            dma((n_t - 1,)),
            dma((n_t - 1,)),
        ],
        compiler_params=pltpu.CompilerParams(
            collective_id=1, has_side_effects=True, vmem_limit_bytes=60 * 1024 * 1024
        ),
        name="gather_next",
    )(next_tab, panels, next_hidden)
    return next_out, new1[None, None], new2[None, None]


def solution(mesh):
    in_specs = (
        P("dp", "tensor"),
        P("dp", "tensor"),
        P("tensor", "dp", None, None, None),
        P("tensor", None),
        P("tensor", None, None),
        P("tensor", "dp", None, None, None),
        P("tensor", "dp", None, None, None),
        P("dp", "tensor"),
    )
    out_specs = (
        P("dp", "tensor"),
        P("tensor", "dp", None, None, None),
        P("tensor", "dp", None, None, None),
    )
    return jax.shard_map(
        per_device, mesh=mesh, in_specs=in_specs, out_specs=out_specs, check_vma=False
    )
```

time: 783 us -> 235 us (0.30)
  waiting for transfers between devices: 386 us -> 0 us
  local copies, waits for them, and re-layouts: 246 us -> 5.67 us
  Pallas kernels: 0 us -> 223 us
  matrix products: 86.7 us -> 0 us
  loops' own time: 31.5 us -> 0 us
  between operations: 13.9 us -> 0.66 us
  other arithmetic: 15.7 us -> 3.71 us
    pallas_call x0 -> x2, Pallas kernels: none -> 223 us  [the longest x1 146 us: per_device(): pl.pallas_call(functools.partial(grad_kernel, nz, nx, slots, row_blocks),...]
    reduce_scatter x2 -> x0, waiting for transfers between devices: 207 us -> none  [the longest x1 133 us: per_device(): lax.psum_scatter(outgoing.astype(jnp.bfloat16), 'dp', scatter_dimension=0...]
    all_gather x2 -> x0, waiting for transfers between devices: 178 us -> none  [the longest x1 104 us: per_device(): whole_cot = lax.all_gather(cotangent, 'tensor', axis=1, tiled=True)]
    gather x18 -> x0, local copies, waits for them, and re-layouts: 132 us -> none  [the longest x16 101 us: keep_term(): selected = cot_blocks[:, pattern[:, keep_index]]]
    dot_general x17 -> x0, matrix products: 86.7 us -> none  [the longest x16 69.8 us: keep_term(): jnp.einsum('tfi,tfj->fij', hidden_blocks, selected, preferred_element_typ...]
    scatter x1 -> x0, local copies, waits for them, and re-layouts: 36 us -> none  [per_device(): dense = dense.at[row_index, pattern].set(packed)]
    another operation x1 -> x0, loops' own time: 31.5 us -> none  [per_device(): terms = lax.map(keep_term, jnp.arange(keep_count, dtype=jnp.int32))]
    while x3 -> x0, local copies, waits for them, and re-layouts: 18.6 us -> none  [per_device(): terms = lax.map(keep_term, jnp.arange(keep_count, dtype=jnp.int32))]
  transfers between devices with their start and end apart: 4 -> 0, of which waited for: 4 -> 0; matrix products, arithmetic and copies ran while one was open for 2% -> 0% of each run, Pallas kernels for 0% -> 0%
where the time goes in v1:
time: 235 us; the launch traced here: 233 us
  Pallas kernels  223 us (95%)
  local copies, waits for them, and re-layouts  5.67 us (2%)
  other arithmetic  3.71 us (2%)
    pallas_call x1, Pallas kernels, per_device(): pl.pallas_call(functools.partial(grad_kernel, nz, nx, slots, row_blocks),...  146 us
    pallas_call x1, Pallas kernels, per_device(): pl.pallas_call(functools.partial(next_kernel, nz, nx, slots, row_blocks),...  77.6 us
    unnamed x3, local copies, waits for them, and re-layouts  5.51 us

profile of v1, /device:TPU:1, one launch (start us, length us, event | category | flops | bytes accessed | tf_op | source)
XLA Modules:
  0.0 233.3 jit_solution(17932033433685590258)
XLA Ops:
  0.6 0.7 broadcast_multiply_fusion
  1.3 0.1 mul.31
  1.4 0.7 reduce
  2.1 0.1 reshape.55
  2.2 0.6 convert_reduce_fusion.1.cnt
  2.8 0.2 convert_reduce_fusion
  3.0 0.1 select_reduce_fusion.1
  3.2 0.6 broadcast_add_fusion.tab
  3.8 0.1 select_reduce_fusion
  3.9 0.6 broadcast_add_fusion.1.tab
  4.5 145.6 %grad_adam.1 = (f32[10,128,128]{2,1,0:T(8,128)}, f32[10,128,128]{2,1,0:T(8,128)}, bf16[10,128,128]{2,1,0:T(8,128)(2,1)}) custom-call(s32[320]{0:T(512)} %broadcast_add_fusion.tab, s32[32]{0:T(128)} %convert_reduce_fusion.1.cnt, bf16[1024,1792]{1,0:T(8,128)(2,1)} %hid.1, bf16[1024,512]{1,0:T(8,128)(2,1)} %cot.1, bf16[10,128,128]{2,1,0:T(8,128)(2,1)} %bitcast.9, ...), custom_call_target="tpu_custom_call" | custom-call | tf_op jit(solution)/shard_map/grad_adam/pallas_call | solution.py:412
  150.2 77.6 %gather_next.1 = bf16[128,512]{1,0:T(8,128)(2,1)} custom-call(s32[448]{0:T(512)} %broadcast_add_fusion.1.tab, bf16[10,128,128]{2,1,0:T(8,128)(2,1)} %get-tuple-element.6.panel, bf16[128,1792]{1,0:T(8,128)(2,1)} %nxt.1), custom_call_target="tpu_custom_call" | custom-call | tf_op jit(solution)/shard_map/gather_next/pallas_call | solution.py:448
  227.8 1.6 copy.14
  229.4 2.0 copy.15
  231.3 2.0 copy.16
  (1 shorter events, 0.0 us)

commit v2 on v1

v2 whole, which is shorter than its diff:
```python
import functools

import jax
import jax.numpy as jnp
from jax import lax
from jax.experimental import pallas as pl
from jax.experimental.pallas import tpu as pltpu
from jax.sharding import PartitionSpec as P

ADAM_STEP = 20
BETA_ONE = 0.9
BETA_TWO = 0.95
LEARN_RATE = 0.003
EPSILON = 1e-08

BLK = 128
CHUNKS = 4
ZF = 2
MESH = pl.DeviceIdType.MESH
f32 = jnp.float32
bf16 = jnp.bfloat16


def remote(src, dst, send, recv, where):
    return pltpu.make_async_remote_copy(
        src_ref=src, dst_ref=dst, send_sem=send, recv_sem=recv, device_id=where, device_id_type=MESH
    )


def greet(places):
    barrier = pltpu.get_barrier_semaphore()
    for where in places:
        pl.semaphore_signal(barrier, inc=1, device_id=where, device_id_type=MESH)
    pl.semaphore_wait(barrier, len(places))


class Place:
    def __init__(self, nz, nx):
        self.nz, self.nx = nz, nx
        self.d = lax.axis_index("dp")
        self.t = lax.axis_index("tensor")
        self.z = lax.div(self.d, 4)
        self.yl = lax.rem(lax.div(self.d, 2), 2)
        self.core = lax.rem(self.d, 2)
        self.x = lax.div(self.t, 2)
        self.yh = lax.rem(self.t, 2)

    def dp_of(self, z, yl, core):
        return (z * 2 + yl) * 2 + core

    def tensor_of(self, x, yh):
        return x * 2 + yh

    def x_step(self, k):
        return lax.rem(self.x + (k + self.nx), self.nx)

    def z_step(self, k):
        return lax.rem(self.z + (k + self.nz), self.nz)


def grad_kernel(
    nz, nx, slots, row_blocks,
    tab, cnt, hid, cot, wgt, m1, m2,
    new1, new2, panels,
    cotbuf, dense, acc, sendb, recvb, ringb, ybuf, yrecv,
    ys, yr, xs, xr, fs, fr, os, orr, ds, dr, rs, rr, ps, pr, ls, lr,
):
    me = Place(nz, nx)
    tokens = cot.shape[0]
    rows = tokens // CHUNKS
    half = rows // 2
    early = tokens // 2
    n_dense = dense.shape[0] - 1
    hs = slots // 2

    y_far = {"tensor": me.tensor_of(me.x, 1 - me.yh)}
    x_next = [{"tensor": me.tensor_of(me.x_step(1), me.yh)}, {"tensor": me.tensor_of(me.x_step(-1), me.yh)}]
    z_next = [{"dp": me.dp_of(me.z_step(1), me.yl, me.core)}, {"dp": me.dp_of(me.z_step(-1), me.yl, me.core)}]
    y_near = {"dp": me.dp_of(me.z, 1 - me.yl, me.core)}
    twin = {"dp": me.dp_of(me.z, me.yl, 1 - me.core)}
    greet([y_far] + x_next + z_next + [y_near, twin])

    t_item = [me.t, me.tensor_of(me.x, 1 - me.yh)]
    x_opp = me.x_step(2)
    t_opp = [me.tensor_of(x_opp, me.yh), me.tensor_of(x_opp, 1 - me.yh)]

    def t_from(item, q):
        yh = me.yh if item == 0 else 1 - me.yh
        return me.tensor_of(me.x_step(-1 if q == 0 else 1), yh)

    def ycopy(c):
        r = pl.ds(c * rows, rows)
        return remote(cot.at[r], cotbuf.at[me.t, r], ys.at[c], yr.at[c], y_far)

    def xcopy(item, q, c):
        r = pl.ds(c * rows, rows)
        src = cot.at[r] if item == 0 else cotbuf.at[t_item[1], r]
        return remote(src, cotbuf.at[t_item[item], r], xs.at[item, q, c], xr.at[item, q, c], x_next[q])

    def fcopy(q, c):
        r = pl.ds(c * rows + q * half, half)
        there = cotbuf.at[t_from(0, q), r]
        return remote(there, there, fs.at[q, c], fr.at[q, c], x_next[q])

    def ocopy(q, c):
        r = pl.ds(c * rows + q * half, half)
        there = cotbuf.at[t_opp[0], r]
        return remote(there, there, os.at[q, c], orr.at[q, c], y_far)

    def group(src, tq, lo=0, hi=tokens, keep=None, plus=None):
        for i in range(row_blocks // 2):
            wide = slice(i * 256, (i + 1) * 256)
            out = lax.dot_general(
                hid[lo:hi, wide], src[lo:hi, :], (((0,), (0,)), ((), ())), preferred_element_type=f32
            )
            if plus is not None:
                out = out + acc[plus, wide, :]
            if keep is not None:
                acc[keep, wide, :] = out
                continue
            for b in range(4):
                for a in range(2):
                    dense[(tq * 4 + b) * row_blocks + 2 * i + a] = out[
                        a * BLK : (a + 1) * BLK, b * BLK : (b + 1) * BLK
                    ].astype(bf16)

    queue = [functools.partial(xcopy, 0, c=0), functools.partial(xcopy, 0, c=1)]
    for c in range(CHUNKS):
        queue.append(functools.partial(fcopy, c=c))
        if c + 2 < CHUNKS:
            queue.append(functools.partial(xcopy, 0, c=c + 2))
        if c == CHUNKS - 2:
            queue.append(functools.partial(xcopy, 1, c=0))
    queue += [functools.partial(xcopy, 1, c=c) for c in range(1, CHUNKS)]

    def go(k):
        for q in range(2):
            queue[k](q=q).start()

    def got(k):
        for q in range(2):
            queue[k](q=q).wait_recv()
        if k + 2 < len(queue):
            go(k + 2)

    def across(c):
        for q in range(2):
            ocopy(q, c).start()

    go(0)
    ycopy(0).start()
    go(1)
    ycopy(1).start()
    dense[n_dense] = jnp.zeros((BLK, BLK), bf16)
    group(cot, me.t)
    got(0)
    ycopy(0).wait_recv()
    ycopy(2).start()
    got(1)
    ycopy(1).wait_recv()
    got(2)
    across(0)
    got(3)
    ycopy(2).wait_recv()
    ycopy(3).start()
    got(4)
    across(1)
    got(5)
    group(cotbuf.at[t_from(0, 0)], t_from(0, 0))
    got(6)
    across(2)
    group(cotbuf.at[t_from(0, 1)], t_from(0, 1))
    ycopy(3).wait_recv()
    got(7)
    group(cotbuf.at[t_item[1]], t_item[1])
    got(8)
    across(3)
    group(cotbuf.at[t_opp[0]], t_opp[0])
    got(9)
    for q in range(2):
        group(cotbuf.at[t_from(1, q)], None, hi=early, keep=q)
    for q in range(2):
        for c in range(CHUNKS):
            ocopy(q, c).wait_recv()
    got(10)
    group(cotbuf.at[t_opp[1]], t_opp[1])
    got(11)
    for q in range(2):
        group(cotbuf.at[t_from(1, q)], t_from(1, q), lo=early, plus=q)

    yf = hs - ZF
    order = [(0, i) for i in range(ZF, hs)] + [(0, i) for i in range(ZF)] + [(1, i) for i in range(hs)]
    part = [(yf, hs), (hs, hs + ZF), (hs + ZF, 2 * hs)]

    def dest_z(s, q):
        return lax.rem(me.z + (2 * nz - 1 - s), nz) if q == 0 else lax.rem(me.z + 1 + s, nz)

    def pick(s, q, p, core):
        u, i = order[p]
        yl = 1 - me.yl if u == 0 else me.yl
        return dense[tab[me.dp_of(dest_z(s, q), yl, core) * slots + q * hs + i]]

    def dcopy(s, q):
        return remote(sendb.at[s, q], recvb.at[s, q], ds.at[s, q], dr.at[s, q], twin)

    def pcopy(s, q):
        return remote(recvb.at[s, q, pl.ds(0, yf)], ybuf.at[s, q], ps.at[s, q], pr.at[s, q], y_near)

    def rcopy(s, q, n):
        lo, hi = part[n]
        return remote(
            recvb.at[s, q, pl.ds(lo, hi - lo)], ringb.at[s, q, pl.ds(lo - yf, hi - lo)],
            rs.at[s, q, n], rr.at[s, q, n], z_next[q],
        )

    def lcopy(q):
        return remote(recvb.at[nz - 1, q, pl.ds(yf, ZF)], yrecv.at[q], ls.at[q], lr.at[q], y_near)

    def fill(s):
        for q in range(2):
            for p in range(2 * hs):
                sendb[s, q, p] = pick(s, q, p, 1 - me.core)
            dcopy(s, q).start()

    def spread(s):
        for q in range(2):
            dcopy(s, q).wait_recv()
            for p in range(yf):
                recvb[s, q, p] = (recvb[s, q, p].astype(f32) + pick(s, q, p, me.core).astype(f32)).astype(bf16)
            pcopy(s, q).start()

    def add(s, q, n, first):
        lo, hi = part[n]
        for p in range(lo, hi):
            v = recvb[s, q, p].astype(f32) + pick(s, q, p, me.core).astype(f32)
            if n == 2:
                v = v + ybuf[s, q, p - lo].astype(f32)
            if not first:
                v = v + ringb[s - 1, q, p - yf].astype(f32)
            recvb[s, q, p] = v.astype(bf16)

    fill(0)
    fill(1)
    spread(0)
    fill(2)
    for n in range(2):
        for q in range(2):
            add(0, q, n, True)
            rcopy(0, q, n).start()
    spread(1)
    fill(3)
    for q in range(2):
        pcopy(0, q).wait_recv()
        add(0, q, 2, True)
        rcopy(0, q, 2).start()

    def hop(s):
        for n in range(3):
            for q in range(2):
                rcopy(s - 1, q, n).wait_recv()
                if n == 2:
                    pcopy(s, q).wait_recv()
                add(s, q, n, False)
                rcopy(s, q, n).start()

    def ring(s, carry):
        spread(s + 1)
        fill(s + 3)
        hop(s)
        return carry

    lax.fori_loop(1, nz - 3, ring, 0)
    for s in range(nz - 3, nz - 1):
        spread(s + 1)
        hop(s)
    for n in range(3):
        for q in range(2):
            rcopy(nz - 2, q, n).wait_recv()
            if n == 2:
                pcopy(nz - 1, q).wait_recv()
            add(nz - 1, q, n, False)
            if n == 0:
                lcopy(q).start()

    scale_one = 1.0 - BETA_ONE**ADAM_STEP
    scale_two = 1.0 - BETA_TWO**ADAM_STEP
    mine = cnt[me.d]

    def adam(q, i):
        k = q * hs + i
        grad = recvb[nz - 1, q, hs + i].astype(f32)
        if i < ZF:
            grad = grad + yrecv[q, i].astype(f32)
        used = k < mine
        one = jnp.where(used, BETA_ONE * m1[k] + (1 - BETA_ONE) * grad, 0.0)
        two = jnp.where(used, BETA_TWO * m2[k] + (1 - BETA_TWO) * grad * grad, 0.0)
        new1[k] = one
        new2[k] = two
        step = LEARN_RATE * (one / scale_one) / (jnp.sqrt(two / scale_two) + EPSILON)
        panels[k] = (wgt[k].astype(f32) - step).astype(bf16)

    for q in range(2):
        for i in range(ZF, hs):
            adam(q, i)
    for q in range(2):
        lcopy(q).wait_recv()
        for i in range(ZF):
            adam(q, i)

    for c in range(CHUNKS):
        ycopy(c).wait_send()
        for q in range(2):
            for item in range(2):
                xcopy(item, q, c).wait_send()
            fcopy(q, c).wait_send()
            ocopy(q, c).wait_send()
    for q in range(2):
        lcopy(q).wait_send()

    def drain(s, carry):
        for q in range(2):
            dcopy(s, q).wait_send()
            pcopy(s, q).wait_send()
        return carry

    def drain_ring(s, carry):
        for q in range(2):
            for n in range(3):
                rcopy(s, q, n).wait_send()
        return carry

    lax.fori_loop(0, nz, drain, 0)
    lax.fori_loop(0, nz - 1, drain_ring, 0)


def next_kernel(
    nz, nx, slots, row_blocks,
    tab, panel, nxt,
    out,
    pan, wide, outb, rcv,
    ys, yr, ps, pr, rs, rr, ds, dr, es, er, ts, tr,
):
    me = Place(nz, nx)
    nt = 2 * nx
    hs = slots // 2
    n_pan = nz * 4 * slots

    z_next = [{"dp": me.dp_of(me.z_step(1), me.yl, me.core)}, {"dp": me.dp_of(me.z_step(-1), me.yl, me.core)}]
    y_near = {"dp": me.dp_of(me.z, 1 - me.yl, me.core)}
    twin = {"dp": me.dp_of(me.z, me.yl, 1 - me.core)}
    peers = [{"tensor": lax.rem(me.t + 1 + m, nt)} for m in range(nt - 1)]
    greet(z_next + [y_near, twin] + peers)

    def place(s, q, u, lo, n):
        z = lax.rem(me.z + (2 * nz - s), nz) if q == 0 else lax.rem(me.z + s, nz)
        yl = me.yl if u == 0 else 1 - me.yl
        return pan.at[pl.ds(me.dp_of(z, yl, me.core) * slots + q * hs + lo, n)]

    def ycopy(q):
        return remote(panel.at[pl.ds(q * hs, ZF)], place(0, q, 0, 0, ZF), ys.at[q], yr.at[q], y_near)

    def pcopy(s, q):
        here = place(s, q, 0, ZF, hs - ZF)
        return remote(here, here, ps.at[s, q], pr.at[s, q], y_near)

    pieces = [(0, 0, ZF), (0, ZF, hs - ZF), (1, 0, ZF)]

    def rcopy(s, q, n):
        here = place(s, q, *pieces[n])
        return remote(here, here, rs.at[s, q, n], rr.at[s, q, n], z_next[q])

    def dcopy(s, q, u):
        here = place(s, q, u, 0, hs if u == 0 else ZF)
        return remote(here, here, ds.at[s, q, u], dr.at[s, q, u], twin)

    def ecopy(s, q):
        here = place(s, q, 1, ZF, hs - ZF)
        return remote(here, here, es.at[s, q], er.at[s, q], twin)

    for q in range(2):
        ycopy(q).start()
    for i in range(slots):
        pan[me.d * slots + i] = panel[i]
    for n in range(2):
        for q in range(2):
            rcopy(0, q, n).start()
    for q in range(2):
        pcopy(0, q).start()
        dcopy(0, q, 0).start()
    pan[n_pan] = jnp.zeros((BLK, BLK), bf16)
    for q in range(2):
        ycopy(q).wait_recv()
        rcopy(0, q, 2).start()
        dcopy(0, q, 1).start()

    def hop(s, last):
        for q in range(2):
            rcopy(s - 1, q, 1).wait_recv()
            if not last:
                rcopy(s, q, 1).start()
            pcopy(s, q).start()
        for q in range(2):
            rcopy(s - 1, q, 0).wait_recv()
            if not last:
                rcopy(s, q, 0).start()
            dcopy(s, q, 0).start()
        for q in range(2):
            rcopy(s - 1, q, 2).wait_recv()
            if not last:
                rcopy(s, q, 2).start()
            dcopy(s, q, 1).start()
        for q in range(2):
            pcopy(s - 1, q).wait_recv()
            ecopy(s - 1, q).start()

    def ring(s, carry):
        hop(s, False)
        return carry

    lax.fori_loop(1, nz - 1, ring, 0)
    hop(nz - 1, True)
    for q in range(2):
        pcopy(nz - 1, q).wait_recv()
        ecopy(nz - 1, q).start()

    def landed(s, carry):
        for q in range(2):
            dcopy(s, q, 0).wait_recv()
            dcopy(s, q, 1).wait_recv()
            ecopy(s, q).wait_recv()
        return carry

    lax.fori_loop(0, nz, landed, 0)

    def tcopy(m):
        return remote(outb.at[m], rcv.at[m], ts.at[m], tr.at[m], peers[m])

    total = None
    for m in range(nt):
        tq = lax.rem(me.t + 1 + m, nt)
        buf = m % 2

        def build(h, carry):
            for b in range(4):
                for i in range(row_blocks // 2):
                    f = h * (row_blocks // 2) + i
                    wide[buf, pl.ds(f * BLK, BLK), b * BLK : (b + 1) * BLK] = pan[tab[(tq * 4 + b) * row_blocks + f]]
            return carry

        lax.fori_loop(0, 2, build, 0)
        part = jnp.dot(nxt[...], wide[buf], preferred_element_type=f32)
        if m < nt - 1:
            outb[m] = part.astype(bf16)
            tcopy(m).start()
        else:
            total = part
    for m in range(nt - 1):
        tcopy(m).wait_recv()
        total = total + rcv[m].astype(f32)
    out[...] = total.astype(bf16)

    for m in range(nt - 1):
        tcopy(m).wait_send()
    for q in range(2):
        ycopy(q).wait_send()

    def drain(s, carry):
        for u in range(2):
            for q in range(2):
                dcopy(s, q, u).wait_send()
        for q in range(2):
            pcopy(s, q).wait_send()
            ecopy(s, q).wait_send()
        return carry

    def drain_ring(s, carry):
        for n in range(3):
            for q in range(2):
                rcopy(s, q, n).wait_send()
        return carry

    lax.fori_loop(0, nz, drain, 0)
    lax.fori_loop(0, nz - 1, drain_ring, 0)


def tables(pattern, owners, dp_devices, slots, row_blocks, col_blocks):
    keep = pattern.shape[1]
    total = row_blocks * keep
    owner = owners.reshape(total)
    number = jnp.arange(total, dtype=jnp.int32)
    same = owner[:, None] == owner[None, :]
    earlier = number[None, :] < number[:, None]
    position = jnp.sum((same & earlier).astype(jnp.int32), axis=1)
    target = owner * slots + position
    where = pattern.reshape(total) * row_blocks + number // keep
    places = jnp.arange(dp_devices * slots, dtype=jnp.int32)
    hit = target[None, :] == places[:, None]
    n_dense = row_blocks * col_blocks
    grad_tab = n_dense + jnp.sum(jnp.where(hit, where[None, :] - n_dense, 0), axis=1)
    spots = jnp.arange(n_dense, dtype=jnp.int32)
    found = where[None, :] == spots[:, None]
    n_pan = dp_devices * slots
    next_tab = n_pan + jnp.sum(jnp.where(found, target[None, :] - n_pan, 0), axis=1)
    people = jnp.arange(dp_devices, dtype=jnp.int32)
    count = jnp.sum((owner[None, :] == people[:, None]).astype(jnp.int32), axis=1)
    return grad_tab, next_tab, count


def per_device(hidden, cotangent, weight_slots, pattern, owners, first_moment, second_moment, next_hidden):
    tokens, width = hidden.shape
    cols = cotangent.shape[1]
    row_blocks = pattern.shape[0]
    slots = first_moment.shape[2]
    n_dp, n_t = lax.axis_size("dp"), lax.axis_size("tensor")
    nz, nx = n_dp // 4, n_t // 2
    col_blocks = cols * n_t // BLK
    hs = slots // 2
    grad_tab, next_tab, count = tables(pattern, owners, n_dp, slots, row_blocks, col_blocks)

    vmem = pl.BlockSpec(memory_space=pltpu.VMEM)
    smem = pl.BlockSpec(memory_space=pltpu.SMEM)
    dma = pltpu.SemaphoreType.DMA
    block = (slots, BLK, BLK)
    new1, new2, panels = pl.pallas_call(
        functools.partial(grad_kernel, nz, nx, slots, row_blocks),
        out_shape=(
            jax.ShapeDtypeStruct(block, f32),
            jax.ShapeDtypeStruct(block, f32),
            jax.ShapeDtypeStruct(block, bf16),
        ),
        in_specs=[smem, smem] + [vmem] * 5,
        out_specs=(vmem, vmem, vmem),
        scratch_shapes=[
            pltpu.VMEM((n_t, tokens, cols), bf16),
            pltpu.VMEM((row_blocks * col_blocks + 1, BLK, BLK), bf16),
            pltpu.VMEM((2, width, cols), f32),
            pltpu.VMEM((nz, 2, slots, BLK, BLK), bf16),
            pltpu.VMEM((nz, 2, slots, BLK, BLK), bf16),
            pltpu.VMEM((nz - 1, 2, hs + ZF, BLK, BLK), bf16),
            pltpu.VMEM((nz, 2, hs - ZF, BLK, BLK), bf16),
            pltpu.VMEM((2, ZF, BLK, BLK), bf16),
            dma((CHUNKS,)),
            dma((CHUNKS,)),
            dma((2, 2, CHUNKS)),
            dma((2, 2, CHUNKS)),
            dma((2, CHUNKS)),
            dma((2, CHUNKS)),
            dma((2, CHUNKS)),
            dma((2, CHUNKS)),
            dma((nz, 2)),
            dma((nz, 2)),
            dma((nz - 1, 2, 3)),
            dma((nz - 1, 2, 3)),
            dma((nz, 2)),
            dma((nz, 2)),
            dma((2,)),
            dma((2,)),
        ],
        compiler_params=pltpu.CompilerParams(
            collective_id=0, has_side_effects=True, vmem_limit_bytes=60 * 1024 * 1024
        ),
        name="grad_adam",
    )(grad_tab, count, hidden, cotangent, weight_slots[0, 0], first_moment[0, 0], second_moment[0, 0])

    next_out = pl.pallas_call(
        functools.partial(next_kernel, nz, nx, slots, row_blocks),
        out_shape=jax.ShapeDtypeStruct((next_hidden.shape[0], cols), bf16),
        in_specs=[smem, vmem, vmem],
        out_specs=vmem,
        scratch_shapes=[
            pltpu.VMEM((n_dp * slots + 1, BLK, BLK), bf16),
            pltpu.VMEM((2, width, cols), bf16),
            pltpu.VMEM((n_t - 1, next_hidden.shape[0], cols), bf16),
            pltpu.VMEM((n_t - 1, next_hidden.shape[0], cols), bf16),
            dma((2,)),
            dma((2,)),
            dma((nz, 2)),
            dma((nz, 2)),
            dma((nz - 1, 2, 3)),
            dma((nz - 1, 2, 3)),
            dma((nz, 2, 2)),
            dma((nz, 2, 2)),
            dma((nz, 2)),
            dma((nz, 2)),
            dma((n_t - 1,)),
            dma((n_t - 1,)),
        ],
        compiler_params=pltpu.CompilerParams(
            collective_id=1, has_side_effects=True, vmem_limit_bytes=60 * 1024 * 1024
        ),
        name="gather_next",
    )(next_tab, panels, next_hidden)
    return next_out, new1[None, None], new2[None, None]


def solution(mesh):
    in_specs = (
        P("dp", "tensor"),
        P("dp", "tensor"),
        P("tensor", "dp", None, None, None),
        P("tensor", None),
        P("tensor", None, None),
        P("tensor", "dp", None, None, None),
        P("tensor", "dp", None, None, None),
        P("dp", "tensor"),
    )
    out_specs = (
        P("dp", "tensor"),
        P("tensor", "dp", None, None, None),
        P("tensor", "dp", None, None, None),
    )
    return jax.shard_map(
        per_device, mesh=mesh, in_specs=in_specs, out_specs=out_specs, check_vma=False
    )
```

time: 235 us -> 193 us (0.82)
  Pallas kernels: 223 us -> 182 us
    pallas_call x1, Pallas kernels: 146 us -> 117 us  [per_device(): pl.pallas_call(functools.partial(grad_kernel, nz, nx, slots, row_blocks),...]
    pallas_call x1, Pallas kernels: 77.6 us -> 65.4 us  [per_device(): pl.pallas_call(functools.partial(next_kernel, nz, nx, slots, row_blocks),...]
where the time goes in v2:
time: 193 us; the launch traced here: 192 us
  Pallas kernels  182 us (94%)
  local copies, waits for them, and re-layouts  5.67 us (3%)
  other arithmetic  3.71 us (2%)
    pallas_call x1, Pallas kernels, per_device(): pl.pallas_call(functools.partial(grad_kernel, nz, nx, slots, row_blocks),...  117 us
    pallas_call x1, Pallas kernels, per_device(): pl.pallas_call(functools.partial(next_kernel, nz, nx, slots, row_blocks),...  65.4 us
    unnamed x3, local copies, waits for them, and re-layouts  5.51 us

profile of v2, /device:TPU:1, one launch (start us, length us, event | category | flops | bytes accessed | tf_op | source)
XLA Modules:
  0.0 192.3 jit_solution(9951324842725668235)
XLA Ops:
  0.6 0.7 broadcast_multiply_fusion
  1.3 0.1 mul.31
  1.4 0.7 reduce
  2.1 0.1 reshape.55
  2.2 0.6 convert_reduce_fusion.1.cnt
  2.8 0.2 convert_reduce_fusion
  3.0 0.1 select_reduce_fusion.1
  3.2 0.6 broadcast_add_fusion.tab
  3.8 0.1 select_reduce_fusion
  3.9 0.6 broadcast_add_fusion.1.tab
  4.5 116.8 %grad_adam.1 = (f32[10,128,128]{2,1,0:T(8,128)}, f32[10,128,128]{2,1,0:T(8,128)}, bf16[10,128,128]{2,1,0:T(8,128)(2,1)}) custom-call(s32[320]{0:T(512)} %broadcast_add_fusion.tab, s32[32]{0:T(128)} %convert_reduce_fusion.1.cnt, bf16[1024,1792]{1,0:T(8,128)(2,1)} %hid.1, bf16[1024,512]{1,0:T(8,128)(2,1)} %cot.1, bf16[10,128,128]{2,1,0:T(8,128)(2,1)} %bitcast.9, ...), custom_call_target="tpu_custom_call" | custom-call | tf_op jit(solution)/shard_map/grad_adam/pallas_call | solution.py:524
  121.3 65.4 %gather_next.1 = bf16[128,512]{1,0:T(8,128)(2,1)} custom-call(s32[448]{0:T(512)} %broadcast_add_fusion.1.tab, bf16[10,128,128]{2,1,0:T(8,128)(2,1)} %get-tuple-element.6.panel, bf16[128,1792]{1,0:T(8,128)(2,1)} %nxt.1), custom_call_target="tpu_custom_call" | custom-call | tf_op jit(solution)/shard_map/gather_next/pallas_call | solution.py:565
  186.8 1.6 copy.14
  188.3 2.0 %copy.15 = f32[1,1,10,128,128]{4,3,2,1,0:T(8,128)} copy(f32[1,1,10,128,128]{4,3,2,1,0:T(8,128)} %bitcast.8) | data formatting | bytes 1310720
  190.3 2.0 %copy.16 = f32[1,1,10,128,128]{4,3,2,1,0:T(8,128)} copy(f32[1,1,10,128,128]{4,3,2,1,0:T(8,128)} %bitcast.7) | data formatting | bytes 1310720
  (1 shorter events, 0.0 us)

commit v3 on v2

v3 whole, which is shorter than its diff:
```python
import functools

import jax
import jax.numpy as jnp
from jax import lax
from jax.experimental import pallas as pl
from jax.experimental.pallas import tpu as pltpu
from jax.sharding import PartitionSpec as P

ADAM_STEP = 20
BETA_ONE = 0.9
BETA_TWO = 0.95
LEARN_RATE = 0.003
EPSILON = 1e-08

BLK = 128
CHUNKS = 4

ZF = 2
MESH = pl.DeviceIdType.MESH
f32 = jnp.float32
bf16 = jnp.bfloat16


def remote(src, dst, send, recv, where):
    return pltpu.make_async_remote_copy(
        src_ref=src, dst_ref=dst, send_sem=send, recv_sem=recv, device_id=where, device_id_type=MESH
    )


def greet(places):
    barrier = pltpu.get_barrier_semaphore()
    for where in places:
        pl.semaphore_signal(barrier, inc=1, device_id=where, device_id_type=MESH)
    pl.semaphore_wait(barrier, len(places))


class Place:
    def __init__(self, nz, nx):
        self.nz, self.nx = nz, nx
        self.d = lax.axis_index("dp")
        self.t = lax.axis_index("tensor")
        self.z = lax.div(self.d, 4)
        self.yl = lax.rem(lax.div(self.d, 2), 2)
        self.core = lax.rem(self.d, 2)
        self.x = lax.div(self.t, 2)
        self.yh = lax.rem(self.t, 2)

    def dp_of(self, z, yl, core):
        return (z * 2 + yl) * 2 + core

    def tensor_of(self, x, yh):
        return x * 2 + yh

    def x_step(self, k):
        return lax.rem(self.x + (k + self.nx), self.nx)

    def z_step(self, k):
        return lax.rem(self.z + (k + self.nz), self.nz)


def moments(grad, used, one, two):
    one = jnp.where(used, BETA_ONE * one + (1 - BETA_ONE) * grad, 0.0)
    two = jnp.where(used, BETA_TWO * two + (1 - BETA_TWO) * grad * grad, 0.0)
    return one, two


def kernel(
    nz, nx, slots, row_blocks,
    tab, cot, hid_in, wgt_in, m1_in, m2_in, nxt_in,
    out, grads,
    hid, wgt, m1, m2, nxt,
    cotbuf, dense, acc, sendb, recvb, ringb, ybuf, yrecv, outb, rcv,
    ins, free,
    ys, yr, xs, xr, fs, fr, os, orr,
    ds, dr, rs, rr, ps, pr, ls, lr,
    ys2, yr2, ps2, pr2, rs2, rr2, ds2, dr2, es, er, ts, tr,
):
    me = Place(nz, nx)
    nt = 2 * nx
    tokens = cot.shape[0]
    width = hid.shape[1]
    rows = tokens // CHUNKS
    half = rows // 2
    early = tokens // 2
    n_dense = dense.shape[0] - 1
    n_slots = nz * 4 * slots
    hs = slots // 2

    loads = [
        pltpu.make_async_copy(src, dst, ins.at[i])
        for i, (src, dst) in enumerate([(hid_in, hid), (wgt_in, wgt), (m1_in, m1), (m2_in, m2), (nxt_in, nxt)])
    ]
    for load in loads:
        load.start()

    y_far = {"tensor": me.tensor_of(me.x, 1 - me.yh)}
    x_next = [{"tensor": me.tensor_of(me.x_step(1), me.yh)}, {"tensor": me.tensor_of(me.x_step(-1), me.yh)}]
    z_next = [{"dp": me.dp_of(me.z_step(1), me.yl, me.core)}, {"dp": me.dp_of(me.z_step(-1), me.yl, me.core)}]
    y_near = {"dp": me.dp_of(me.z, 1 - me.yl, me.core)}
    twin = {"dp": me.dp_of(me.z, me.yl, 1 - me.core)}
    near = z_next + [y_near, twin]
    away = [(2, 1), (1, 1), (nx - 1, 1), (0, 1), (2, 0), (1, 0), (nx - 1, 0)]
    t_away = [me.tensor_of(me.x_step(dx), 1 - me.yh if far else me.yh) for dx, far in away] + [me.t]
    peers = [{"tensor": t_away[m]} for m in range(nt - 1)]
    greet(near + peers)

    t_item = [me.t, me.tensor_of(me.x, 1 - me.yh)]
    x_opp = me.x_step(2)
    t_opp = [me.tensor_of(x_opp, me.yh), me.tensor_of(x_opp, 1 - me.yh)]

    def t_from(item, q):
        yh = me.yh if item == 0 else 1 - me.yh
        return me.tensor_of(me.x_step(-1 if q == 0 else 1), yh)

    def held(t, lo, n):
        return cotbuf.at[pl.ds(t * tokens + lo, n)]

    def ycopy(c):
        return remote(cot.at[pl.ds(c * rows, rows)], held(me.t, c * rows, rows), ys.at[c], yr.at[c], y_far)

    def xcopy(item, q, c):
        there = held(t_item[item], c * rows, rows)
        src = cot.at[pl.ds(c * rows, rows)] if item == 0 else there
        return remote(src, there, xs.at[item, q, c], xr.at[item, q, c], x_next[q])

    def fcopy(q, c):
        there = held(t_from(0, q), c * rows + q * half, half)
        return remote(there, there, fs.at[q, c], fr.at[q, c], x_next[q])

    def ocopy(q, c):
        there = held(t_opp[0], c * rows + q * half, half)
        return remote(there, there, os.at[q, c], orr.at[q, c], y_far)

    def group(src, tq, lo=0, hi=tokens, keep=None, plus=None):
        for i in range(row_blocks // 2):
            wide = slice(i * 256, (i + 1) * 256)
            got_here = lax.dot_general(
                hid[lo:hi, wide], src[lo:hi, :], (((0,), (0,)), ((), ())), preferred_element_type=f32
            )
            if plus is not None:
                got_here = got_here + acc[plus, wide, :]
            if keep is not None:
                acc[keep, wide, :] = got_here
                continue
            for b in range(4):
                for a in range(2):
                    dense[(tq * 4 + b) * row_blocks + 2 * i + a] = got_here[
                        a * BLK : (a + 1) * BLK, b * BLK : (b + 1) * BLK
                    ].astype(bf16)

    def group_of(t, **how):
        group(held(t, 0, tokens), t, **how)

    queue = [functools.partial(xcopy, 0, c=0), functools.partial(xcopy, 0, c=1)]
    for c in range(CHUNKS):
        queue.append(functools.partial(fcopy, c=c))
        if c + 2 < CHUNKS:
            queue.append(functools.partial(xcopy, 0, c=c + 2))
        if c == CHUNKS - 2:
            queue.append(functools.partial(xcopy, 1, c=0))
    queue += [functools.partial(xcopy, 1, c=c) for c in range(1, CHUNKS)]

    def go(k):
        for q in range(2):
            queue[k](q=q).start()

    def got(k):
        for q in range(2):
            queue[k](q=q).wait_recv()
        if k + 2 < len(queue):
            go(k + 2)

    def across(c):
        for q in range(2):
            ocopy(q, c).start()

    go(0)
    ycopy(0).start()
    go(1)
    ycopy(1).start()
    dense[n_dense] = jnp.zeros((BLK, BLK), bf16)
    loads[0].wait()
    group(cot, me.t)
    got(0)
    ycopy(0).wait_recv()
    ycopy(2).start()
    got(1)
    ycopy(1).wait_recv()
    got(2)
    across(0)
    got(3)
    ycopy(2).wait_recv()
    ycopy(3).start()
    got(4)
    across(1)
    got(5)
    group_of(t_from(0, 0))
    got(6)
    across(2)
    group_of(t_from(0, 1))
    ycopy(3).wait_recv()
    got(7)
    group_of(t_item[1])
    got(8)
    across(3)
    group_of(t_opp[0])
    got(9)
    for q in range(2):
        group_of(t_from(1, q), hi=early, keep=q)
    for q in range(2):
        for c in range(CHUNKS):
            ocopy(q, c).wait_recv()
    got(10)
    group_of(t_opp[1])
    got(11)
    for q in range(2):
        group_of(t_from(1, q), lo=early, plus=q)

    yf = hs - ZF
    order = [(0, i) for i in range(ZF, hs)] + [(0, i) for i in range(ZF)] + [(1, i) for i in range(hs)]
    part = [(yf, hs), (hs, hs + ZF), (hs + ZF, 2 * hs)]

    def dest_z(s, q):
        return lax.rem(me.z + (2 * nz - 1 - s), nz) if q == 0 else lax.rem(me.z + 1 + s, nz)

    def pick(s, q, p, core):
        u, i = order[p]
        yl = 1 - me.yl if u == 0 else me.yl
        return dense[tab[me.dp_of(dest_z(s, q), yl, core) * slots + q * hs + i]]

    def dcopy(s, q):
        return remote(sendb.at[s, q], recvb.at[s, q], ds.at[s, q], dr.at[s, q], twin)

    def pcopy(s, q):
        return remote(recvb.at[s, q, pl.ds(0, yf)], ybuf.at[s, q], ps.at[s, q], pr.at[s, q], y_near)

    def rcopy(s, q, n):
        lo, hi = part[n]
        return remote(
            recvb.at[s, q, pl.ds(lo, hi - lo)], ringb.at[s, q, pl.ds(lo - yf, hi - lo)],
            rs.at[s, q, n], rr.at[s, q, n], z_next[q],
        )

    def lcopy(q):
        return remote(recvb.at[nz - 1, q, pl.ds(yf, ZF)], yrecv.at[q], ls.at[q], lr.at[q], y_near)

    def fill(s):
        for q in range(2):
            for p in range(2 * hs):
                sendb[s, q, p] = pick(s, q, p, 1 - me.core)
            dcopy(s, q).start()

    def spread(s):
        for q in range(2):
            dcopy(s, q).wait_recv()
            for p in range(yf):
                recvb[s, q, p] = (recvb[s, q, p].astype(f32) + pick(s, q, p, me.core).astype(f32)).astype(bf16)
            pcopy(s, q).start()

    def add(s, q, n, first=False):
        lo, hi = part[n]
        for p in range(lo, hi):
            v = recvb[s, q, p].astype(f32) + pick(s, q, p, me.core).astype(f32)
            if n == 2:
                v = v + ybuf[s, q, p - lo].astype(f32)
            if not first:
                v = v + ringb[s - 1, q, p - yf].astype(f32)
            recvb[s, q, p] = v.astype(bf16)

    def hop_ahead(s):
        for n in range(2):
            for q in range(2):
                rcopy(s - 1, q, n).wait_recv()
                add(s, q, n)
                rcopy(s, q, n).start()

    def hop_behind(s):
        for q in range(2):
            rcopy(s - 1, q, 2).wait_recv()
            pcopy(s, q).wait_recv()
            add(s, q, 2)
            rcopy(s, q, 2).start()

    fill(0)
    fill(1)
    spread(0)
    fill(2)
    for n in range(2):
        for q in range(2):
            add(0, q, n, True)
            rcopy(0, q, n).start()
    spread(1)
    fill(3)
    hop_ahead(1)
    for q in range(2):
        pcopy(0, q).wait_recv()
        add(0, q, 2, True)
        rcopy(0, q, 2).start()

    def ring(s, carry):
        spread(s)
        fill(s + 2)
        hop_ahead(s)
        hop_behind(s - 1)
        return carry

    lax.fori_loop(2, nz - 2, ring, 0)
    spread(nz - 2)
    hop_ahead(nz - 2)
    hop_behind(nz - 3)
    spread(nz - 1)
    for n in range(2):
        for q in range(2):
            rcopy(nz - 2, q, n).wait_recv()
            add(nz - 1, q, n)
            if n == 0:
                lcopy(q).start()
    hop_behind(nz - 2)
    for q in range(2):
        rcopy(nz - 2, q, 2).wait_recv()
        pcopy(nz - 1, q).wait_recv()
        add(nz - 1, q, 2)

    for where in near:
        pl.semaphore_signal(free, inc=1, device_id=where, device_id_type=MESH)

    pan = dense
    scale_one = 1.0 - BETA_ONE**ADAM_STEP
    scale_two = 1.0 - BETA_TWO**ADAM_STEP
    mine = tab[n_slots + n_dense]
    for load in loads[1:]:
        load.wait()

    def adam(q, i):
        k = q * hs + i
        grad = recvb[nz - 1, q, hs + i].astype(f32)
        if i < ZF:
            grad = grad + yrecv[q, i].astype(f32)
        grads[k] = grad
        one, two = moments(grad, k < mine, m1[k], m2[k])
        step = LEARN_RATE * (one / scale_one) / (jnp.sqrt(two / scale_two) + EPSILON)
        pan[me.d * slots + k] = (wgt[k].astype(f32) - step).astype(bf16)

    for q in range(2):
        for i in range(ZF, hs):
            adam(q, i)
    pl.semaphore_wait(free, len(near))

    def place(s, q, u, lo, n):
        z = lax.rem(me.z + (2 * nz - s), nz) if q == 0 else lax.rem(me.z + s, nz)
        yl = me.yl if u == 0 else 1 - me.yl
        return pan.at[pl.ds(me.dp_of(z, yl, me.core) * slots + q * hs + lo, n)]

    pieces = [(0, 0, ZF), (0, ZF, hs - ZF), (1, 0, ZF)]

    def ycopy2(q):
        here = place(0, q, 0, 0, ZF)
        return remote(here, here, ys2.at[q], yr2.at[q], y_near)

    def pcopy2(s, q):
        here = place(s, q, 0, ZF, hs - ZF)
        return remote(here, here, ps2.at[s, q], pr2.at[s, q], y_near)

    def rcopy2(s, q, n):
        here = place(s, q, *pieces[n])
        return remote(here, here, rs2.at[s, q, n], rr2.at[s, q, n], z_next[q])

    def dcopy2(s, q, u):
        here = place(s, q, u, 0, hs if u == 0 else ZF)
        return remote(here, here, ds2.at[s, q, u], dr2.at[s, q, u], twin)

    def ecopy2(s, q):
        here = place(s, q, 1, ZF, hs - ZF)
        return remote(here, here, es.at[s, q], er.at[s, q], twin)

    for q in range(2):
        rcopy2(0, q, 1).start()
        pcopy2(0, q).start()
    for q in range(2):
        lcopy(q).wait_recv()
        for i in range(ZF):
            adam(q, i)
        ycopy2(q).start()
        rcopy2(0, q, 0).start()
        dcopy2(0, q, 0).start()

    def ahead2(s, last=False):
        for q in range(2):
            rcopy2(s - 1, q, 1).wait_recv()
            if not last:
                rcopy2(s, q, 1).start()
            pcopy2(s, q).start()

    def behind2(s, last=False):
        for n, u in ((0, 0), (2, 1)):
            for q in range(2):
                rcopy2(s - 1, q, n).wait_recv()
                if not last:
                    rcopy2(s, q, n).start()
                dcopy2(s, q, u).start()

    def landed2(s):
        for q in range(2):
            pcopy2(s, q).wait_recv()
            ecopy2(s, q).start()

    ahead2(1)
    for q in range(2):
        ycopy2(q).wait_recv()
        rcopy2(0, q, 2).start()
        dcopy2(0, q, 1).start()
    landed2(0)

    def ring2(s, carry):
        ahead2(s)
        behind2(s - 1)
        landed2(s - 1)
        return carry

    lax.fori_loop(2, nz - 1, ring2, 0)
    ahead2(nz - 1, True)
    behind2(nz - 2)
    landed2(nz - 2)

    for c in range(CHUNKS):
        ycopy(c).wait_send()
        for q in range(2):
            for item in range(2):
                xcopy(item, q, c).wait_send()
            fcopy(q, c).wait_send()
            ocopy(q, c).wait_send()

    behind2(nz - 1, True)
    landed2(nz - 1)

    def all_here(s, carry):
        for q in range(2):
            dcopy2(s, q, 0).wait_recv()
            dcopy2(s, q, 1).wait_recv()
            ecopy2(s, q).wait_recv()
        return carry

    lax.fori_loop(0, nz, all_here, 0)

    def tcopy(m):
        return remote(outb.at[m], rcv.at[m], ts.at[m], tr.at[m], peers[m])

    total = None
    for m in range(nt):
        tq = t_away[m]
        lo = (m % 2) * width

        def build(h, carry):
            for b in range(4):
                for i in range(row_blocks // 2):
                    f = h * (row_blocks // 2) + i
                    cotbuf[pl.ds(lo + f * BLK, BLK), b * BLK : (b + 1) * BLK] = pan[tab[n_slots + (tq * 4 + b) * row_blocks + f]]
            return carry

        lax.fori_loop(0, 2, build, 0)
        piece = jnp.dot(nxt[...], cotbuf[lo : lo + width, :], preferred_element_type=f32)
        if m < nt - 1:
            outb[m] = piece.astype(bf16)
            tcopy(m).start()
        else:
            total = piece
    for m in range(nt - 1):
        tcopy(m).wait_recv()
        total = total + rcv[m].astype(f32)
    out[...] = total

    for m in range(nt - 1):
        tcopy(m).wait_send()
    for q in range(2):
        lcopy(q).wait_send()
        ycopy2(q).wait_send()

    def drain(s, carry):
        for q in range(2):
            dcopy(s, q).wait_send()
            pcopy(s, q).wait_send()
            dcopy2(s, q, 0).wait_send()
            dcopy2(s, q, 1).wait_send()
            ecopy2(s, q).wait_send()
            pcopy2(s, q).wait_send()
        return carry

    def drain_ring(s, carry):
        for q in range(2):
            for n in range(3):
                rcopy(s, q, n).wait_send()
                rcopy2(s, q, n).wait_send()
        return carry

    lax.fori_loop(0, nz, drain, 0)
    lax.fori_loop(0, nz - 1, drain_ring, 0)


def table(pattern, owners, dp_devices, slots, row_blocks, col_blocks):
    keep = pattern.shape[1]
    total = row_blocks * keep
    n_dense = row_blocks * col_blocks
    n_slots = dp_devices * slots
    owner = owners.reshape(total)
    number = jnp.arange(total, dtype=jnp.int32)
    same = owner[:, None] == owner[None, :]
    earlier = number[None, :] < number[:, None]
    target = owner * slots + jnp.sum((same & earlier).astype(jnp.int32), axis=1)
    where = pattern.reshape(total) * row_blocks + number // keep
    row = jnp.arange(n_slots + n_dense + 1, dtype=jnp.int32)[:, None]
    first, last = row < n_slots, row == n_slots + n_dense
    mine = owner == lax.axis_index("dp")
    hit = jnp.where(first, target[None, :] == row, jnp.where(last, mine[None, :], where[None, :] == row - n_slots))
    value = jnp.where(first, where[None, :] - n_dense, jnp.where(last, 1, target[None, :] - n_dense))
    return jnp.where(last[:, 0], 0, n_dense) + jnp.sum(jnp.where(hit, value, 0), axis=1)


def finish_kernel(cnt, total, grads, m1, m2, out, new1, new2):
    out[...] = total[...].astype(bf16)
    for k in range(grads.shape[0]):
        new1[k], new2[k] = moments(grads[k], k < cnt[cnt.shape[0] - 1], m1[k], m2[k])


def per_device(hidden, cotangent, weight_slots, pattern, owners, first_moment, second_moment, next_hidden):
    tokens, width = hidden.shape
    cols = cotangent.shape[1]
    row_blocks = pattern.shape[0]
    slots = first_moment.shape[2]
    n_dp, n_t = lax.axis_size("dp"), lax.axis_size("tensor")
    nz, nx = n_dp // 4, n_t // 2
    col_blocks = cols * n_t // BLK
    hs = slots // 2
    next_rows = next_hidden.shape[0]
    tab = table(pattern, owners, n_dp, slots, row_blocks, col_blocks)

    vmem = pl.BlockSpec(memory_space=pltpu.VMEM)
    smem = pl.BlockSpec(memory_space=pltpu.SMEM)
    anywhere = pl.BlockSpec(memory_space=pl.ANY)
    dma = pltpu.SemaphoreType.DMA
    block = (slots, BLK, BLK)

    def pairs(*shapes):
        return [dma(shape) for shape in shapes for _ in range(2)]

    next_out, grads = pl.pallas_call(
        functools.partial(kernel, nz, nx, slots, row_blocks),
        out_shape=(
            jax.ShapeDtypeStruct((next_rows, cols), f32),
            jax.ShapeDtypeStruct(block, f32),
        ),
        in_specs=[smem, vmem] + [anywhere] * 5,
        out_specs=(vmem, vmem),
        scratch_shapes=[
            pltpu.VMEM((tokens, width), bf16),
            pltpu.VMEM(block, bf16),
            pltpu.VMEM(block, f32),
            pltpu.VMEM(block, f32),
            pltpu.VMEM((next_rows, width), bf16),
            pltpu.VMEM((n_t * tokens, cols), bf16),
            pltpu.VMEM((row_blocks * col_blocks + 1, BLK, BLK), bf16),
            pltpu.VMEM((2, width, cols), f32),
            pltpu.VMEM((nz, 2, slots, BLK, BLK), bf16),
            pltpu.VMEM((nz, 2, slots, BLK, BLK), bf16),
            pltpu.VMEM((nz - 1, 2, hs + ZF, BLK, BLK), bf16),
            pltpu.VMEM((nz, 2, hs - ZF, BLK, BLK), bf16),
            pltpu.VMEM((2, ZF, BLK, BLK), bf16),
            pltpu.VMEM((n_t - 1, next_rows, cols), bf16),
            pltpu.VMEM((n_t - 1, next_rows, cols), bf16),
            dma((5,)),
            pltpu.SemaphoreType.REGULAR,
        ]
        + pairs((CHUNKS,), (2, 2, CHUNKS), (2, CHUNKS), (2, CHUNKS))
        + pairs((nz, 2), (nz - 1, 2, 3), (nz, 2), (2,))
        + pairs((2,), (nz, 2), (nz - 1, 2, 3), (nz, 2, 2), (nz, 2), (n_t - 1,)),
        compiler_params=pltpu.CompilerParams(
            collective_id=0, has_side_effects=True, vmem_limit_bytes=60 * 1024 * 1024
        ),
        name="step",
    )(
        tab, cotangent,
        hidden, weight_slots[0, 0], first_moment[0, 0], second_moment[0, 0], next_hidden,
    )
    next_out, new1, new2 = pl.pallas_call(
        finish_kernel,
        out_shape=(
            jax.ShapeDtypeStruct((next_rows, cols), bf16),
            jax.ShapeDtypeStruct(block, f32),
            jax.ShapeDtypeStruct(block, f32),
        ),
        in_specs=[smem] + [vmem] * 4,
        out_specs=(vmem, vmem, vmem),
        name="finish",
    )(tab, next_out, grads, first_moment[0, 0], second_moment[0, 0])
    return next_out, new1[None, None], new2[None, None]


def solution(mesh):
    in_specs = (
        P("dp", "tensor"),
        P("dp", "tensor"),
        P("tensor", "dp", None, None, None),
        P("tensor", None),
        P("tensor", None, None),
        P("tensor", "dp", None, None, None),
        P("tensor", "dp", None, None, None),
        P("dp", "tensor"),
    )
    out_specs = (
        P("dp", "tensor"),
        P("tensor", "dp", None, None, None),
        P("tensor", "dp", None, None, None),
    )
    return jax.shard_map(
        per_device, mesh=mesh, in_specs=in_specs, out_specs=out_specs, check_vma=False
    )
```

time: 193 us -> 182 us (0.943)
  local copies, waits for them, and re-layouts: 5.67 us -> 0.16 us
  Pallas kernels: 182 us -> 179 us
    unnamed x3 -> x0, local copies, waits for them, and re-layouts: 5.51 us -> none
    pallas_call x2, Pallas kernels: 182 us -> 179 us  [the longest x1 176 us: per_device(): pl.pallas_call(functools.partial(kernel, nz, nx, slots, row_blocks), out_...]
where the time goes in v3:
time: 182 us
  Pallas kernels  179 us (98%)
  other arithmetic  2.78 us (2%)
    pallas_call x1, Pallas kernels, per_device(): pl.pallas_call(functools.partial(kernel, nz, nx, slots, row_blocks), out_...  176 us

profile of v3, /device:TPU:1, one launch (start us, length us, event | category | flops | bytes accessed | tf_op | source)
XLA Modules:
  0.0 182.2 jit_solution(5120050519642438494)
XLA Ops:
  0.7 0.7 broadcast_multiply_fusion
  1.4 0.1 mul.33
  1.4 0.7 reduce
  2.2 0.1 reshape.76
  2.3 0.2 convert_reduce_fusion
  2.4 0.6 select_reduce_fusion
  3.0 0.6 select_add_fusion.tab.cnt
  3.6 175.8 %step.1 = (f32[128,512]{1,0:T(8,128)}, f32[10,128,128]{2,1,0:T(8,128)}) custom-call(s32[769]{0:T(1024)} %select_add_fusion.tab.cnt, bf16[1024,512]{1,0:T(8,128)(2,1)} %cot.1, bf16[1024,1792]{1,0:T(8,128)(2,1)} %hid_in.1, bf16[10,128,128]{2,1,0:T(8,128)(2,1)} %bitcast.9, f32[10,128,128]{2,1,0:T(8,128)} %bitcast.5, f32[10,128,128]{2,1,0:T(8,128)} %bitcast.7, ...), custom_call_target="tpu_custom_call" | custom-call | tf_op jit(solution)/shard_map/step/pallas_call | solution.py:546
  179.4 2.8 %finish.1 = (bf16[128,512]{1,0:T(8,128)(2,1)}, f32[10,128,128]{2,1,0:T(8,128)}, f32[10,128,128]{2,1,0:T(8,128)}) custom-call(s32[769]{0:T(1024)} %select_add_fusion.tab.cnt, f32[128,512]{1,0:T(8,128)} %get-tuple-element.8.total, f32[10,128,128]{2,1,0:T(8,128)} %get-tuple-element.9.grads, f32[10,128,128]{2,1,0:T(8,128)} %bitcast.6, f32[10,128,128]{2,1,0:T(8,128)} %bitcast.8), custom_call_target="tpu_custom_call" | custom-call | tf_op jit(solution)/shard_map/finish/pallas_call | solution.py:584
  (4 shorter events, 0.0 us)

commit v4 on v3

--- a/solution.py
+++ b/solution.py
@@ -28,10 +28,12 @@
     )
 
 
-def greet(places):
+def greet(places, loads):
     barrier = pltpu.get_barrier_semaphore()
     for where in places:
         pl.semaphore_signal(barrier, inc=1, device_id=where, device_id_type=MESH)
+    for load in loads:
+        load.start()
     pl.semaphore_wait(barrier, len(places))
 
 
@@ -67,12 +69,12 @@
 
 def kernel(
     nz, nx, slots, row_blocks,
-    tab, cot, hid_in, wgt_in, m1_in, m2_in, nxt_in,
+    tab_in, cot, hid_in, wgt_in, m1_in, m2_in, nxt_in,
     out, grads,
-    hid, wgt, m1, m2, nxt,
+    tab, hid, wgt, m1, m2, nxt,
     cotbuf, dense, acc, sendb, recvb, ringb, ybuf, yrecv, outb, rcv,
     ins, free,
-    ys, yr, xs, xr, fs, fr, os, orr,
+    ys, yr, xs, xr, fs, fr, os, orr, gs, gr,
     ds, dr, rs, rr, ps, pr, ls, lr,
     ys2, yr2, ps2, pr2, rs2, rr2, ds2, dr2, es, er, ts, tr,
 ):
@@ -82,18 +84,15 @@
     width = hid.shape[1]
     rows = tokens // CHUNKS
     half = rows // 2
-    early = tokens // 2
+    early, late = tokens // 2, tokens - rows
+    last = CHUNKS - 1
     n_dense = dense.shape[0] - 1
     n_slots = nz * 4 * slots
     hs = slots // 2
 
-    loads = [
-        pltpu.make_async_copy(src, dst, ins.at[i])
-        for i, (src, dst) in enumerate([(hid_in, hid), (wgt_in, wgt), (m1_in, m1), (m2_in, m2), (nxt_in, nxt)])
-    ]
-    for load in loads:
-        load.start()
-
+    own = cotbuf.at[pl.ds(me.t * tokens, tokens)]
+    moves = [(cot, own), (hid_in, hid), (tab_in, tab), (wgt_in, wgt), (m1_in, m1), (m2_in, m2), (nxt_in, nxt)]
+    loads = [pltpu.make_async_copy(src, dst, ins.at[i]) for i, (src, dst) in enumerate(moves)]
     y_far = {"tensor": me.tensor_of(me.x, 1 - me.yh)}
     x_next = [{"tensor": me.tensor_of(me.x_step(1), me.yh)}, {"tensor": me.tensor_of(me.x_step(-1), me.yh)}]
     z_next = [{"dp": me.dp_of(me.z_step(1), me.yl, me.core)}, {"dp": me.dp_of(me.z_step(-1), me.yl, me.core)}]
@@ -103,7 +102,7 @@
     away = [(2, 1), (1, 1), (nx - 1, 1), (0, 1), (2, 0), (1, 0), (nx - 1, 0)]
     t_away = [me.tensor_of(me.x_step(dx), 1 - me.yh if far else me.yh) for dx, far in away] + [me.t]
     peers = [{"tensor": t_away[m]} for m in range(nt - 1)]
-    greet(near + peers)
+    greet(near + peers, loads)
 
     t_item = [me.t, me.tensor_of(me.x, 1 - me.yh)]
     x_opp = me.x_step(2)
@@ -120,7 +119,7 @@
         return remote(cot.at[pl.ds(c * rows, rows)], held(me.t, c * rows, rows), ys.at[c], yr.at[c], y_far)
 
     def xcopy(item, q, c):
-        there = held(t_item[item], c * rows, rows)
+        there = held(t_item[item], c * rows, half if item == 1 and c == last else rows)
         src = cot.at[pl.ds(c * rows, rows)] if item == 0 else there
         return remote(src, there, xs.at[item, q, c], xr.at[item, q, c], x_next[q])
 
@@ -131,6 +130,10 @@
     def ocopy(q, c):
         there = held(t_opp[0], c * rows + q * half, half)
         return remote(there, there, os.at[q, c], orr.at[q, c], y_far)
+
+    def gcopy(q):
+        there = held(t_from(0, q), last * rows + half, half)
+        return remote(there, there, gs.at[q], gr.at[q], y_far)
 
     def group(src, tq, lo=0, hi=tokens, keep=None, plus=None):
         for i in range(row_blocks // 2):
@@ -180,8 +183,9 @@
     go(1)
     ycopy(1).start()
     dense[n_dense] = jnp.zeros((BLK, BLK), bf16)
-    loads[0].wait()
-    group(cot, me.t)
+    for load in loads[:3]:
+        load.wait()
+    group(own, me.t)
     got(0)
     ycopy(0).wait_recv()
     ycopy(2).start()
@@ -195,6 +199,8 @@
     got(4)
     across(1)
     got(5)
+    for q in range(2):
+        gcopy(q).start()
     group_of(t_from(0, 0))
     got(6)
     across(2)
@@ -211,11 +217,14 @@
     for q in range(2):
         for c in range(CHUNKS):
             ocopy(q, c).wait_recv()
+    group_of(t_opp[1])
     got(10)
-    group_of(t_opp[1])
+    for q in range(2):
+        group_of(t_from(1, q), lo=early, hi=late, keep=q, plus=q)
     got(11)
     for q in range(2):
-        group_of(t_from(1, q), lo=early, plus=q)
+        gcopy(q).wait_recv()
+        group_of(t_from(1, q), lo=late, plus=q)
 
     yf = hs - ZF
     order = [(0, i) for i in range(ZF, hs)] + [(0, i) for i in range(ZF)] + [(1, i) for i in range(hs)]
@@ -329,7 +338,7 @@
     scale_one = 1.0 - BETA_ONE**ADAM_STEP
     scale_two = 1.0 - BETA_TWO**ADAM_STEP
     mine = tab[n_slots + n_dense]
-    for load in loads[1:]:
+    for load in loads[3:]:
         load.wait()
 
     def adam(q, i):
@@ -430,6 +439,8 @@
                 xcopy(item, q, c).wait_send()
             fcopy(q, c).wait_send()
             ocopy(q, c).wait_send()
+    for q in range(2):
+        gcopy(q).wait_send()
 
     behind2(nz - 1, True)
     landed2(nz - 1)
@@ -502,13 +513,13 @@
     total = row_blocks * keep
     n_dense = row_blocks * col_blocks
     n_slots = dp_devices * slots
-    owner = owners.reshape(total)
+    owner = lax.optimization_barrier(owners.reshape(total))
     number = jnp.arange(total, dtype=jnp.int32)
     same = owner[:, None] == owner[None, :]
     earlier = number[None, :] < number[:, None]
     target = owner * slots + jnp.sum((same & earlier).astype(jnp.int32), axis=1)
     where = pattern.reshape(total) * row_blocks + number // keep
-    row = jnp.arange(n_slots + n_dense + 1, dtype=jnp.int32)[:, None]
+    row = jnp.arange(-(-(n_slots + n_dense + 1) // 1024) * 1024, dtype=jnp.int32)[:, None]
     first, last = row < n_slots, row == n_slots + n_dense
     mine = owner == lax.axis_index("dp")
     hit = jnp.where(first, target[None, :] == row, jnp.where(last, mine[None, :], where[None, :] == row - n_slots))
@@ -516,10 +527,10 @@
     return jnp.where(last[:, 0], 0, n_dense) + jnp.sum(jnp.where(hit, value, 0), axis=1)
 
 
-def finish_kernel(cnt, total, grads, m1, m2, out, new1, new2):
+def finish_kernel(n_last, cnt, total, grads, m1, m2, out, new1, new2):
     out[...] = total[...].astype(bf16)
     for k in range(grads.shape[0]):
-        new1[k], new2[k] = moments(grads[k], k < cnt[cnt.shape[0] - 1], m1[k], m2[k])
+        new1[k], new2[k] = moments(grads[k], k < cnt[n_last], m1[k], m2[k])
 
 
 def per_device(hidden, cotangent, weight_slots, pattern, owners, first_moment, second_moment, next_hidden):
@@ -549,9 +560,10 @@
             jax.ShapeDtypeStruct((next_rows, cols), f32),
             jax.ShapeDtypeStruct(block, f32),
         ),
-        in_specs=[smem, vmem] + [anywhere] * 5,
+        in_specs=[anywhere] * 7,
         out_specs=(vmem, vmem),
         scratch_shapes=[
+            pltpu.SMEM(tab.shape, jnp.int32),
             pltpu.VMEM((tokens, width), bf16),
             pltpu.VMEM(block, bf16),
             pltpu.VMEM(block, f32),
@@ -567,10 +579,10 @@
             pltpu.VMEM((2, ZF, BLK, BLK), bf16),
             pltpu.VMEM((n_t - 1, next_rows, cols), bf16),
             pltpu.VMEM((n_t - 1, next_rows, cols), bf16),
-            dma((5,)),
+            dma((7,)),
             pltpu.SemaphoreType.REGULAR,
         ]
-        + pairs((CHUNKS,), (2, 2, CHUNKS), (2, CHUNKS), (2, CHUNKS))
+        + pairs((CHUNKS,), (2, 2, CHUNKS), (2, CHUNKS), (2, CHUNKS), (2,))
         + pairs((nz, 2), (nz - 1, 2, 3), (nz, 2), (2,))
         + pairs((2,), (nz, 2), (nz - 1, 2, 3), (nz, 2, 2), (nz, 2), (n_t - 1,)),
         compiler_params=pltpu.CompilerParams(
@@ -582,7 +594,7 @@
         hidden, weight_slots[0, 0], first_moment[0, 0], second_moment[0, 0], next_hidden,
     )
     next_out, new1, new2 = pl.pallas_call(
-        finish_kernel,
+        functools.partial(finish_kernel, n_dp * slots + row_blocks * col_blocks),
         out_shape=(
             jax.ShapeDtypeStruct((next_rows, cols), bf16),
             jax.ShapeDtypeStruct(block, f32),

time: 182 us -> 179 us (0.984)
  Pallas kernels: 179 us -> 175 us
    pallas_call x1, Pallas kernels: 176 us -> 173 us  [per_device(): pl.pallas_call(functools.partial(kernel, nz, nx, slots, row_blocks), out_...]
where the time goes in v4:
time: 179 us
  Pallas kernels  175 us (98%)
  other arithmetic  2.69 us (2%)
    pallas_call x1, Pallas kernels, per_device(): pl.pallas_call(functools.partial(kernel, nz, nx, slots, row_blocks), out_...  173 us

profile of v4, /device:TPU:1, one launch (start us, length us, event | category | flops | bytes accessed | tf_op | source)
XLA Modules:
  0.0 178.9 jit_solution(10943895506028843744)
XLA Ops:
  0.7 0.7 broadcast_multiply_fusion
  1.4 0.1 mul.26
  1.4 0.7 reduce
  2.2 0.1 reshape.60
  2.3 0.2 convert_reduce_fusion
  2.4 0.5 select_reduce_fusion
  2.9 0.6 select_add_fusion.tab_in.cnt
  3.5 172.5 %step.1 = (f32[128,512]{1,0:T(8,128)}, f32[10,128,128]{2,1,0:T(8,128)}) custom-call(s32[1024]{0:T(1024)} %select_add_fusion.tab_in.cnt, bf16[1024,512]{1,0:T(8,128)(2,1)} %cot.1, bf16[1024,1792]{1,0:T(8,128)(2,1)} %hid_in.1, bf16[10,128,128]{2,1,0:T(8,128)(2,1)} %bitcast.9, f32[10,128,128]{2,1,0:T(8,128)} %bitcast.5, f32[10,128,128]{2,1,0:T(8,128)} %bitcast.7, ...), custom_call_target="tpu_custom_call" | custom-call | tf_op jit(solution)/shard_map/step/pallas_call | solution.py:557
  176.1 2.8 %finish.1 = (bf16[128,512]{1,0:T(8,128)(2,1)}, f32[10,128,128]{2,1,0:T(8,128)}, f32[10,128,128]{2,1,0:T(8,128)}) custom-call(s32[1024]{0:T(1024)} %select_add_fusion.tab_in.cnt, f32[128,512]{1,0:T(8,128)} %get-tuple-element.8.total, f32[10,128,128]{2,1,0:T(8,128)} %get-tuple-element.9.grads, f32[10,128,128]{2,1,0:T(8,128)} %bitcast.6, f32[10,128,128]{2,1,0:T(8,128)} %bitcast.8), custom_call_target="tpu_custom_call" | custom-call | tf_op jit(solution)/shard_map/finish/pallas_call | solution.py:596
  (4 shorter events, 0.0 us)

commit v5 on v4

--- a/solution.py
+++ b/solution.py
@@ -99,7 +99,7 @@
     y_near = {"dp": me.dp_of(me.z, 1 - me.yl, me.core)}
     twin = {"dp": me.dp_of(me.z, me.yl, 1 - me.core)}
     near = z_next + [y_near, twin]
-    away = [(2, 1), (1, 1), (nx - 1, 1), (0, 1), (2, 0), (1, 0), (nx - 1, 0)]
+    away = [(2, 1), (2, 0), (1, 1), (nx - 1, 1), (0, 1), (1, 0), (nx - 1, 0)]
     t_away = [me.tensor_of(me.x_step(dx), 1 - me.yh if far else me.yh) for dx, far in away] + [me.t]
     peers = [{"tensor": t_away[m]} for m in range(nt - 1)]
     greet(near + peers, loads)
@@ -351,10 +351,6 @@
         step = LEARN_RATE * (one / scale_one) / (jnp.sqrt(two / scale_two) + EPSILON)
         pan[me.d * slots + k] = (wgt[k].astype(f32) - step).astype(bf16)
 
-    for q in range(2):
-        for i in range(ZF, hs):
-            adam(q, i)
-    pl.semaphore_wait(free, len(near))
 
     def place(s, q, u, lo, n):
         z = lax.rem(me.z + (2 * nz - s), nz) if q == 0 else lax.rem(me.z + s, nz)
@@ -384,6 +380,10 @@
         return remote(here, here, es.at[s, q], er.at[s, q], twin)
 
     for q in range(2):
+        for i in range(ZF, hs):
+            adam(q, i)
+        if q == 0:
+            pl.semaphore_wait(free, len(near))
         rcopy2(0, q, 1).start()
         pcopy2(0, q).start()
     for q in range(2):

time: 179 us -> 179 us (level)
  no operation moved by 1% of the time
where the time goes in v5:
time: 179 us
  Pallas kernels  175 us (98%)
  other arithmetic  2.69 us (2%)
    pallas_call x1, Pallas kernels, per_device(): pl.pallas_call(functools.partial(kernel, nz, nx, slots, row_blocks), out_...  172 us

profile of v5, /device:TPU:1, one launch (start us, length us, event | category | flops | bytes accessed | tf_op | source)
XLA Modules:
  0.0 178.8 jit_solution(15838085385900085043)
XLA Ops:
  0.7 0.7 broadcast_multiply_fusion
  1.4 0.1 mul.26
  1.4 0.7 reduce
  2.2 0.1 reshape.60
  2.3 0.2 convert_reduce_fusion
  2.4 0.5 select_reduce_fusion
  2.9 0.6 select_add_fusion.tab_in.cnt
  3.5 172.5 %step.1 = (f32[128,512]{1,0:T(8,128)}, f32[10,128,128]{2,1,0:T(8,128)}) custom-call(s32[1024]{0:T(1024)} %select_add_fusion.tab_in.cnt, bf16[1024,512]{1,0:T(8,128)(2,1)} %cot.1, bf16[1024,1792]{1,0:T(8,128)(2,1)} %hid_in.1, bf16[10,128,128]{2,1,0:T(8,128)(2,1)} %bitcast.9, f32[10,128,128]{2,1,0:T(8,128)} %bitcast.5, f32[10,128,128]{2,1,0:T(8,128)} %bitcast.7, ...), custom_call_target="tpu_custom_call" | custom-call | tf_op jit(solution)/shard_map/step/pallas_call | solution.py:557
  176.0 2.8 %finish.1 = (bf16[128,512]{1,0:T(8,128)(2,1)}, f32[10,128,128]{2,1,0:T(8,128)}, f32[10,128,128]{2,1,0:T(8,128)}) custom-call(s32[1024]{0:T(1024)} %select_add_fusion.tab_in.cnt, f32[128,512]{1,0:T(8,128)} %get-tuple-element.8.total, f32[10,128,128]{2,1,0:T(8,128)} %get-tuple-element.9.grads, f32[10,128,128]{2,1,0:T(8,128)} %bitcast.6, f32[10,128,128]{2,1,0:T(8,128)} %bitcast.8), custom_call_target="tpu_custom_call" | custom-call | tf_op jit(solution)/shard_map/finish/pallas_call | solution.py:596
  (4 shorter events, 0.0 us)
